TPU v7x, 32 devices: a whole 2x2x4 slice. The times are simulated.
32 devices in a mesh: groups: 2 (over x), ctx: 4 (over y, core), head: 4 (over z).
Axes of the slice: x: 2, y: 2, z: 4, core: 2. Of those that a mesh axis runs over, the one named last changes fastest.
Arguments:
- cache_latent: bfloat16 [32768, 576], P(('groups', 'ctx')), parts along dimension 0, may hold values from -16 to 16
- index_key: bfloat16 [32768, 128], P(('groups', 'ctx')), parts along dimension 0, may hold values from -6 to 6
- query_latent: bfloat16 [512, 128, 576], P('groups', 'head'), parts along dimension 0, may hold values from -16 to 16
- index_query: bfloat16 [512, 64, 128], P('groups', 'head'), parts along dimension 0, may hold values from -6 to 6
- index_weight: bfloat16 [512, 64], P('groups', 'head'), parts along dimension 0, may hold values from -1 to 1
- block_ids: int32 [512, 32], P('groups'), parts along dimension 0, may hold values from 0 to 255, as said below
- stretch_start: int32 [2], P('groups'), parts along dimension 0, may hold values from 0 to 4095
Outputs:
- index_scores: float32 [32768, 256], P(('groups', 'ctx', 'head')), parts along dimension 0
- attended: bfloat16 [512, 128, 512], P(('groups', 'ctx'), 'head'), parts along dimension 0
There are 2 independent parts, one for each index of `groups`. A program takes and returns all parts, laid end to end along the dimension named above; each array names one. Nothing has to cross between parts.
Inputs may be any that keep to these rules, and one draw needn't show every extreme that they name: `block_ids`: each row names 32 different blocks. Of the segments of 64 blocks (blocks o * 64 to o * 64 + 63), in each row a quarter hold exactly 16 of its blocks, a half hold 8 and a quarter none.
All inputs are finite; a program needn't handle non-finite values.
Results may differ from a plain program's by a relative error of at most 0.005.
Values may be sent and summed in bfloat16 or wider, within the bound.
No kernel may reach another device: no remote copies, remote signals or barrier semaphores. Data moves between devices by JAX's collectives and lax.ppermute only.
A program may use at most 192 MiB of HBM per device.

v0:
```python
import functools

import jax
import jax.numpy as jnp
from jax import lax
from jax.experimental import pallas as pl
from jax.experimental.pallas import tpu as pltpu
from jax.sharding import PartitionSpec as P

LATENT_WIDTH = 512
DR = 64
ID = 128
QKD = 192
BS = 64
NEG = -1e30
EXP_SCALE = QKD**-0.5 * 1.4426950408889634
UNROLL = 4
VMEM_LIMIT = 58 * 2**20


def rope_tables(rows, stretch_start):
    half = DR // 2
    positions = (stretch_start[0] + jnp.arange(rows, dtype=jnp.int32)).astype(jnp.float32)
    freqs = 10000.0 ** (-jnp.arange(half, dtype=jnp.float32) / half)
    angle = positions[None, :] * freqs[:, None]
    return jnp.cos(angle), jnp.sin(angle)


def index_kernel(key_ref, query_ref, weight_ref, out_ref):
    keys = key_ref[...]
    total = None
    for head in range(query_ref.shape[0]):
        product = lax.dot_general(
            keys, query_ref[head], (((1,), (1,)), ((), ())), preferred_element_type=jnp.float32
        )
        term = jnp.maximum(product, 0.0) * weight_ref[head : head + 1, :]
        total = term if total is None else total + term
    out_ref[...] = total


def index_partial(index_key, index_query, index_weight):
    tokens = index_key.shape[0]
    rows, heads, width = index_query.shape
    tile = 256
    query = jnp.transpose(index_query, (1, 0, 2))
    weight = jnp.transpose(index_weight).astype(jnp.float32) * ID ** (-0.5)
    return pl.pallas_call(
        index_kernel,
        grid=(tokens // tile,),
        out_shape=jax.ShapeDtypeStruct((tokens, rows), jnp.float32),
        in_specs=[
            pl.BlockSpec((tile, width), lambda i: (i, 0)),
            pl.BlockSpec((heads, rows, width), lambda i: (0, 0, 0)),
            pl.BlockSpec((heads, rows), lambda i: (0, 0)),
        ],
        out_specs=pl.BlockSpec((tile, rows), lambda i: (i, 0)),
        compiler_params=pltpu.CompilerParams(vmem_limit_bytes=VMEM_LIMIT),
        cost_estimate=pl.CostEstimate(
            flops=4 * tokens * rows * heads * width,
            bytes_accessed=4 * tokens * rows,
            transcendentals=0,
        ),
        name="indexer",
    )(index_key, query, weight)


def attend_kernel(
    chunk,
    groups,
    offset_ref,
    count_ref,
    slot_ref,
    query_hbm,
    cosine_ref,
    sine_ref,
    own_hbm,
    peer_hbm,
    out_ref,
    top_ref,
    total_ref,
    stage_ref,
    turned_ref,
    value_ref,
    raw_ref,
    query_ref,
    part_ref,
    stat_ref,
    item_ref,
    start_ref,
    sems,
):
    rows, heads, width = query_ref.shape
    tokens = own_hbm.shape[1]
    half = DR // 2
    piece = stage_ref.shape[2]
    pieces = 2 * tokens // piece
    offset = offset_ref[0]
    tile = pl.multiple_of(offset // 128 * 128, 128)
    inside = offset - tile

    def cache_copy(number):
        source = own_hbm if number * piece < tokens else peer_hbm
        return pltpu.make_async_copy(
            source.at[:, pl.ds(number * piece % tokens, piece)],
            stage_ref.at[number % 2],
            sems.at[number % 2],
        )

    query_copy = pltpu.make_async_copy(query_hbm.at[:, :, pl.ds(tile, 128)], raw_ref, sems.at[2])
    cache_copy(0).start()
    query_copy.start()
    cache_copy(1).start()

    def list_row(row, filled):
        start_ref[row] = filled
        for part in range(groups):
            item_ref[filled + part] = row * groups + part
        return filled + count_ref[0, offset + row]

    start_ref[rows] = lax.fori_loop(0, rows, list_row, 0)

    low_half = lax.broadcasted_iota(jnp.int32, (width, 2 * BS), 1) < BS

    for number in range(pieces):
        cache_copy(number).wait()

        def turn(index, carry, number=number):
            both = stage_ref[number % 2, :, pl.ds(pl.multiple_of(index * 128, 128), 128)]
            swapped = jnp.concatenate([both[:, BS:], both[:, :BS]], axis=1)
            block = number * (piece // BS) + 2 * index
            turned_ref[block] = jnp.where(low_half, both, swapped)
            turned_ref[block + 1] = jnp.where(low_half, swapped, both)
            values = both[:LATENT_WIDTH].T
            value_ref[block] = values[:BS]
            value_ref[block + 1] = values[BS:]
            return carry

        lax.fori_loop(0, piece // 128, turn, 0)
        if number + 2 < pieces:
            cache_copy(number + 2).start()

    query_copy.wait()
    cosine = cosine_ref[:, pl.ds(tile, 128)]
    sine = sine_ref[:, pl.ds(tile, 128)]

    def turn_query(block, carry):
        for head in range(8):
            raw = raw_ref[block * 8 + head].astype(jnp.float32)
            first = raw[LATENT_WIDTH : LATENT_WIDTH + half]
            second = raw[LATENT_WIDTH + half :]
            rotated = jnp.concatenate(
                [
                    raw[:LATENT_WIDTH],
                    first * cosine - second * sine,
                    second * cosine + first * sine,
                ],
                axis=0,
            ).T
            picked = rotated[:rows]
            for place in range(1, 128 // rows):
                picked = jnp.where(
                    inside == place * rows, rotated[place * rows : (place + 1) * rows], picked
                )
            query_ref[:, block * 8 + head, :] = picked
        return carry

    lax.fori_loop(0, heads // 8, turn_query, 0)

    out_lane = lax.broadcasted_iota(jnp.int32, (heads, 128), 1)
    wide = LATENT_WIDTH // 128
    batch = part_ref.shape[0] // groups

    def attend_batch(number, stats):
        base = start_ref[number * batch]
        stop = start_ref[(number + 1) * batch]

        def step(index, carry):
            done = []
            for unrolled in range(UNROLL):
                item = jnp.minimum(base + index * UNROLL + unrolled, stop - 1)
                code = item_ref[item]
                row = code // groups
                part = code % groups
                names = [slot_ref[part * chunk + j, offset + row] for j in range(chunk)]
                keys = jnp.concatenate(
                    [
                        jnp.where(low_half, turned_ref[names[j]], turned_ref[names[j + 1]])
                        for j in range(0, chunk, 2)
                    ],
                    axis=1,
                )
                values = jnp.concatenate([value_ref[name] for name in names], axis=0)
                scores = jnp.dot(
                    query_ref[row].astype(jnp.bfloat16), keys, preferred_element_type=jnp.float32
                )
                top = jnp.max(scores, axis=1, keepdims=True)
                weights = jnp.exp2((scores - top) * EXP_SCALE)
                total = jnp.sum(weights, axis=1, keepdims=True)
                numer = jnp.dot(
                    weights.astype(jnp.bfloat16), values, preferred_element_type=jnp.float32
                )
                done.append((item - base, numer, top, total))
            for item, numer, top, total in done:
                part_ref[item] = numer
                stat_ref[0, item] = jnp.broadcast_to(top, (heads, 128))
                stat_ref[1, item] = jnp.broadcast_to(total, (heads, 128))
            return carry

        lax.fori_loop(0, (stop - base + UNROLL - 1) // UNROLL, step, 0)

        def merge_row(index, carry):
            tops, totals = carry
            row = number * batch + index
            count = count_ref[0, offset + row]
            first = start_ref[row] - base
            places = [
                jnp.maximum(first + jnp.minimum(part, count - 1), 0) for part in range(groups)
            ]
            peaks = [
                jnp.where(part < count, stat_ref[0, places[part]], NEG) for part in range(groups)
            ]
            peak = functools.reduce(jnp.maximum, peaks)
            factors = [
                jnp.where(part < count, jnp.exp2((peaks[part] - peak) * EXP_SCALE), 0.0)
                for part in range(groups)
            ]
            total = sum(
                jnp.where(part < count, factors[part] * stat_ref[1, places[part]], 0.0)
                for part in range(groups)
            )
            inverse = jnp.where(count > 0, 1.0 / total, 0.0)
            merged = sum(
                jnp.where(
                    part < count,
                    part_ref[places[part]]
                    * jnp.concatenate([factors[part] * inverse] * wide, axis=1),
                    0.0,
                )
                for part in range(groups)
            )
            out_ref[row] = merged.astype(jnp.bfloat16)
            here = out_lane == row
            return jnp.where(here, peak, tops), jnp.where(here, total, totals)

        return lax.fori_loop(0, batch, merge_row, stats)

    blank = jnp.zeros((heads, 128), jnp.float32)
    tops, totals = lax.fori_loop(0, rows // batch, attend_batch, (blank, blank))
    top_ref[...] = tops
    total_ref[...] = totals


def attend(offset, counts, slots, query, cosine, sine, own, peer, rows, chunk, groups):
    heads, width = query.shape[0], query.shape[1]
    tokens = own.shape[1]
    blocks = tokens // BS
    smem = pl.BlockSpec(memory_space=pltpu.SMEM)
    vmem = pl.BlockSpec(memory_space=pltpu.VMEM)
    hbm = pl.BlockSpec(memory_space=pl.ANY)
    batch = min(rows, 32)
    return pl.pallas_call(
        functools.partial(attend_kernel, chunk, groups),
        out_shape=(
            jax.ShapeDtypeStruct((rows, heads, LATENT_WIDTH), jnp.bfloat16),
            jax.ShapeDtypeStruct((heads, 128), jnp.float32),
            jax.ShapeDtypeStruct((heads, 128), jnp.float32),
        ),
        in_specs=[smem, smem, smem, hbm, vmem, vmem, hbm, hbm],
        out_specs=(vmem, vmem, vmem),
        scratch_shapes=[
            pltpu.VMEM((2, width, tokens // 2), jnp.bfloat16),
            pltpu.VMEM((2 * blocks, width, 2 * BS), jnp.bfloat16),
            pltpu.VMEM((2 * blocks, BS, LATENT_WIDTH), jnp.bfloat16),
            pltpu.VMEM((heads, width, 128), jnp.bfloat16),
            pltpu.VMEM((rows, heads, width), jnp.float32),
            pltpu.VMEM((batch * groups, heads, LATENT_WIDTH), jnp.float32),
            pltpu.VMEM((2, batch * groups, heads, 128), jnp.float32),
            pltpu.SMEM((rows * groups + groups,), jnp.int32),
            pltpu.SMEM((rows + 1,), jnp.int32),
            pltpu.SemaphoreType.DMA((3,)),
        ],
        compiler_params=pltpu.CompilerParams(vmem_limit_bytes=VMEM_LIMIT),
        cost_estimate=pl.CostEstimate(
            flops=40 * 10**9, bytes_accessed=16 * 2**20, transcendentals=2 * 10**6
        ),
        name="attend",
    )(offset, counts, slots, query, cosine, sine, own, peer)


def chip_slots(block_ids, own_segment, peer_segment, blocks, chunk, groups):
    ids = jnp.transpose(block_ids)
    segment = ids // blocks
    local = ids % blocks
    place_of = jnp.where(segment == peer_segment, local + blocks, local)
    owned = (segment == own_segment) | (segment == peer_segment)
    count = ids.shape[0]
    before = jnp.tril(jnp.ones((count, count), jnp.float32), -1)
    place = jnp.dot(before, owned.astype(jnp.float32)).astype(jnp.int32)
    place = jnp.where(owned, place, -1)
    wanted = jnp.arange(groups * chunk, dtype=jnp.int32)
    slots = jnp.sum(
        jnp.where(place[:, None, :] == wanted[None, :, None], place_of[:, None, :], 0), axis=0
    )
    counts = jnp.sum(owned.astype(jnp.int32), axis=0, keepdims=True) // chunk
    return counts, slots


def per_device(
    cache_latent, index_key, query_latent, index_query, index_weight, block_ids, stretch_start
):
    shards = lax.axis_size("ctx")
    me = lax.axis_index("ctx")
    pairs = shards // 2
    core = me % 2
    pair = me // 2
    total_rows = query_latent.shape[0]
    rows = total_rows // shards
    chunk = block_ids.shape[1] // shards
    groups = 2 + min(2, shards // 4)
    blocks = cache_latent.shape[0] // BS

    own = jnp.transpose(cache_latent)
    peer = lax.ppermute(own, "ctx", [(i, i ^ 1) for i in range(shards)])
    partial = index_partial(index_key, index_query, index_weight)
    index_scores = lax.psum_scatter(partial, "head", scatter_dimension=0, tiled=True)

    query = jnp.transpose(query_latent, (1, 2, 0))
    cosine, sine = rope_tables(total_rows, stretch_start)
    counts, slots = chip_slots(block_ids, me, me ^ 1, blocks, chunk, groups)

    def attend_for(owner):
        offset = (owner * rows).astype(jnp.int32).reshape(1)
        return attend(
            offset, counts, slots, query, cosine, sine, own, peer, rows, chunk, groups
        )

    parts = []
    for ahead in range(1, pairs):
        owner = ((pair + ahead) % pairs) * 2 + core
        moves = [(i, ((i // 2 + ahead) % pairs) * 2 + i % 2) for i in range(shards)]
        parts.append([lax.ppermute(part, "ctx", moves) for part in attend_for(owner)])
    parts.append(attend_for(me))

    peak = functools.reduce(jnp.maximum, [part[1] for part in parts])
    shares = [jnp.exp2((part[1] - peak) * EXP_SCALE) * part[2] for part in parts]
    whole = sum(shares)
    attended = sum(
        part[0].astype(jnp.float32) * jnp.transpose((share / whole)[:, :rows])[:, :, None]
        for part, share in zip(parts, shares)
    )
    return (index_scores, attended.astype(jnp.bfloat16))


def solution(mesh):
    in_specs = (
        P(("groups", "ctx"), None),
        P(("groups", "ctx"), None),
        P("groups", "head", None),
        P("groups", "head", None),
        P("groups", "head"),
        P("groups", None),
        P("groups"),
    )
    out_specs = (P(("groups", "ctx", "head"), None), P(("groups", "ctx"), "head", None))
    return jax.shard_map(
        per_device, mesh=mesh, in_specs=in_specs, out_specs=out_specs, check_vma=False
    )
```

profile of v0, /device:TPU:28, one launch (start us, length us, event | category | flops | bytes accessed | tf_op | source)
XLA Modules:
  0.0 222.2 jit_solution(6149009785200966064)
XLA Ops:
  7.2 0.0 reduce-scatter.2.cloned.1.call-start
  7.2 0.1 collective-permute-start
  7.3 2.5 %copy.16 = bf16[256,16,128]{2,0,1:T(8,128)(2,1)} copy(bf16[256,16,128]{2,1,0:T(8,128)(2,1)} %param.10) | data formatting | bytes 2097152 | tf_op args[3]
  9.8 1.3 multiply_bitcast_fusion.weight_ref
  11.1 14.9 %indexer.1 = f32[4096,256]{1,0:T(8,128)} custom-call(bf16[4096,128]{1,0:T(8,128)(2,1)} %key_ref.1, bf16[16,256,128]{2,1,0:T(8,128)(2,1)} %bitcast.48, f32[16,256]{1,0:T(8,128)} %multiply_bitcast_fusion.weight_ref), custom_call_target="tpu_custom_call" | custom-call | flops 8589934592 | bytes 4194304 | tf_op jit(solution)/shard_map/indexer/pallas_call | solution.py:47
  26.0 0.0 copy-start
  26.0 0.0 reduce-scatter.2.cloned.1.call-update
  26.7 0.0 copy-done
  26.8 0.1 convert_reduce_fusion
  26.8 0.6 and_select_fusion.count_ref
  27.4 0.2 fusion
  27.6 0.8 multiply_sine_fusion
  28.4 0.7 select_reduce_fusion.slot_ref
  29.2 0.0 collective-permute-done.peer_hbm
  29.2 88.4 %attend.2 = (bf16[64,32,512]{2,1,0:T(8,128)(2,1)}, f32[32,128]{1,0:T(8,128)}, f32[32,128]{1,0:T(8,128)}) custom-call(s32[1]{0:T(128)} %bitcast.2.offset_ref, s32[1,256]{1,0:T(1,128)} %and_select_fusion.count_ref, s32[24,256]{1,0:T(8,128)} %select_reduce_fusion.slot_ref, bf16[32,576,256]{2,1,0:T(8,128)(2,1)} %bitcast.50, ...), custom_call_target="tpu_custom_call" | custom-call | flops 40000000000 | bytes 16777216 | tf_op jit(solution)/shard_map/attend/pallas_call | solution.py:261
  117.6 0.1 collective-permute-start.2
  117.7 2.0 collective-permute-start.3
  119.7 0.1 collective-permute-start.1
  119.8 91.5 %attend.3 = (bf16[64,32,512]{2,1,0:T(8,128)(2,1)}, f32[32,128]{1,0:T(8,128)}, f32[32,128]{1,0:T(8,128)}) custom-call(s32[1]{0:T(128)} %bitcast.8.offset_ref, s32[1,256]{1,0:T(1,128)} %and_select_fusion.count_ref, s32[24,256]{1,0:T(8,128)} %select_reduce_fusion.slot_ref, bf16[32,576,256]{2,1,0:T(8,128)(2,1)} %bitcast.51, ...), custom_call_target="tpu_custom_call" | custom-call | flops 40000000000 | bytes 16777216 | tf_op jit(solution)/shard_map/attend/pallas_call | solution.py:261
  211.2 0.0 collective-permute-done.2
  211.3 0.0 collective-permute-done.3
  211.3 0.8 fusion.18
  212.0 0.1 copy.13
  212.1 0.1 copy.14
  212.2 0.0 collective-permute-done.1
  212.2 3.2 %add_convert_fusion = bf16[64,32,512]{2,1,0:T(8,128)(2,1)} fusion(bf16[64,32,512]{2,1,0:T(8,128)(2,1)} %get-tuple-element.13, bf16[64,32,512]{2,1,0:T(8,128)(2,1)S(1)} %collective-permute-done.1, f32[64,32]{1,0:T(8,128)S(1)} %copy.14, f32[64,32]{1,0:T(8,128)S(1)} %copy.13), kind=kLoop, calls=%fused_computation | loop fusion | flops 6291456 | bytes 6307840 | tf_op jit(solution)/shard_map/convert_element_type | solution.py:351
  215.4 0.0 reduce-scatter.2.cloned.1.call-done
  (4 shorter events, 0.0 us)
Async XLA Ops:
  7.2 208.2 %reduce-scatter.2.cloned.1.call-start = ((), (), s32[]{:S(2)}) async-start(), calls=%async_computation.1 | async-start | bytes 5242880 | tf_op jit(solution)/shard_map/reduce_scatter | solution.py:325
  7.2 22.0 %collective-permute-start = (bf16[576,4096]{1,0:T(8,128)(2,1)}, bf16[576,4096]{1,0:T(8,128)(2,1)}, u32[]{:S(2)}, u32[]{:S(2)}) collective-permute-start(bf16[576,4096]{1,0:T(8,128)(2,1)} %bitcast.52), channel_id=1, source_target_pairs={{0,4},{4,0},{8,12},{12,8},{1,5},{5,1},{9,13},{13,9},{2,6},{6,2},{1... | collective-permute-start | bytes 14155784 | tf_op jit(solution)/shard_map/ppermute | solution.py:323
  26.0 0.8 copy-start
  117.6 93.6 %collective-permute-start.2 = (f32[32,128]{1,0:T(8,128)}, f32[32,128]{1,0:T(8,128)S(1)}, u32[]{:S(2)}, u32[]{:S(2)}) collective-permute-start(f32[32,128]{1,0:T(8,128)} %get-tuple-element.9), channel_id=1, source_target_pairs={{0,8},{4,12},{8,0},{12,4},{1,9},{5,13},{9,1},{13,5},{2,10},{6,14},... | collective-permute-start | bytes 49160 | tf_op jit(solution)/shard_map/ppermute | solution.py:341
  117.7 93.6 %collective-permute-start.3 = (f32[32,128]{1,0:T(8,128)}, f32[32,128]{1,0:T(8,128)S(1)}, u32[]{:S(2)}, u32[]{:S(2)}) collective-permute-start(f32[32,128]{1,0:T(8,128)} %get-tuple-element.11), channel_id=1, source_target_pairs={{0,8},{4,12},{8,0},{12,4},{1,9},{5,13},{9,1},{13,5},{2,10},{6,14},... | collective-permute-start | bytes 49160 | tf_op jit(solution)/shard_map/ppermute | solution.py:341
  119.7 92.5 %collective-permute-start.1 = (bf16[64,32,512]{2,1,0:T(8,128)(2,1)}, bf16[64,32,512]{2,1,0:T(8,128)(2,1)S(1)}, u32[]{:S(2)}, u32[]{:S(2)}) collective-permute-start(bf16[64,32,512]{2,1,0:T(8,128)(2,1)} %get-tuple-element.8), channel_id=1, source_target_pairs={{0,8},{4,12},{8,0},{12,4},{1,9},{5,13},{9,1},{13,5},{2,10},{6,14},... | collective-permute-start | bytes 6291464 | tf_op jit(solution)/shard_map/ppermute | solution.py:341
Sparse Core Ops, SparseCore 0:
  26.2 77.3 reduce-scatter.1
where the time goes:
time: 221 us; the launch traced here: 222 us
  Pallas kernels  195 us (88%)
  between operations  14.8 us (7%)
  other arithmetic  7.46 us (3%)
  local copies, waits for them, and re-layouts  2.67 us (1%)
  starting transfers between devices  2.27 us (1%)
    pallas_call x2, Pallas kernels, attend(): pl.pallas_call(functools.partial(attend_kernel, chunk, groups), out_shape...  180 us
    pallas_call x1, Pallas kernels, index_partial(): pl.pallas_call(index_kernel, grid=(tokens // tile,), out_shape=jax.ShapeD...  14.9 us
  transfers between devices with their start and end apart: 5, of which 0 were waited for; matrix products, arithmetic and copies ran while one was open for 5% of the time, Pallas kernels for 88%

commit v1 on v0

--- a/solution.py
+++ b/solution.py
@@ -14,7 +14,8 @@
 BS = 64
 NEG = -1e30
 EXP_SCALE = QKD**-0.5 * 1.4426950408889634
-UNROLL = 4
+UNROLL = 8
+MERGE = 4
 VMEM_LIMIT = 58 * 2**20
 
 
@@ -26,34 +27,69 @@
     return jnp.cos(angle), jnp.sin(angle)
 
 
-def index_kernel(key_ref, query_ref, weight_ref, out_ref):
-    keys = key_ref[...]
-    total = None
-    for head in range(query_ref.shape[0]):
-        product = lax.dot_general(
-            keys, query_ref[head], (((1,), (1,)), ((), ())), preferred_element_type=jnp.float32
-        )
-        term = jnp.maximum(product, 0.0) * weight_ref[head : head + 1, :]
-        total = term if total is None else total + term
-    out_ref[...] = total
-
-
-def index_partial(index_key, index_query, index_weight):
+def index_kernel(place_ref, key_ref, query_ref, weight_ref, own_ref, sent_ref, wide_ref, turned_ref):
+    del place_ref
+    heads, _, rows = turned_ref.shape
+    share = key_ref.shape[0]
+    step = pl.program_id(0)
+
+    @pl.when(step == 0)
+    def _():
+        wide_ref[...] = query_ref[...].astype(jnp.float32)
+        for head in range(heads):
+            turned_ref[head] = wide_ref[:, head, :].T.astype(jnp.bfloat16)
+
+    weight = weight_ref[...].astype(jnp.float32) * ID ** (-0.5)
+
+    def scores(first, count):
+        keys = key_ref[pl.ds(first, count)]
+        total = None
+        for head in range(heads):
+            product = jnp.dot(keys, turned_ref[head], preferred_element_type=jnp.float32)
+            term = jnp.maximum(product, 0.0) * weight[head : head + 1, :]
+            total = term if total is None else total + term
+        return total
+
+    count = min(share, 128)
+
+    @pl.when(step == 0)
+    def _():
+        for first in range(0, share, count):
+            own_ref[pl.ds(first, count)] = scores(first, count)
+
+    @pl.when(step > 0)
+    def _():
+        for first in range(0, share, count):
+            sent_ref[0, pl.ds(first, count)] = scores(first, count).astype(jnp.bfloat16)
+
+
+def index_partial(index_key, index_query, index_weight, place, shards):
     tokens = index_key.shape[0]
     rows, heads, width = index_query.shape
-    tile = 256
-    query = jnp.transpose(index_query, (1, 0, 2))
-    weight = jnp.transpose(index_weight).astype(jnp.float32) * ID ** (-0.5)
+    share = tokens // shards
     return pl.pallas_call(
         index_kernel,
-        grid=(tokens // tile,),
-        out_shape=jax.ShapeDtypeStruct((tokens, rows), jnp.float32),
-        in_specs=[
-            pl.BlockSpec((tile, width), lambda i: (i, 0)),
-            pl.BlockSpec((heads, rows, width), lambda i: (0, 0, 0)),
-            pl.BlockSpec((heads, rows), lambda i: (0, 0)),
-        ],
-        out_specs=pl.BlockSpec((tile, rows), lambda i: (i, 0)),
+        grid_spec=pltpu.PrefetchScalarGridSpec(
+            num_scalar_prefetch=1,
+            grid=(shards,),
+            in_specs=[
+                pl.BlockSpec((share, width), lambda i, at: (lax.rem(at[0] + i, shards), 0)),
+                pl.BlockSpec((rows, heads, width), lambda i, at: (0, 0, 0)),
+                pl.BlockSpec((heads, rows), lambda i, at: (0, 0)),
+            ],
+            out_specs=(
+                pl.BlockSpec((share, rows), lambda i, at: (0, 0)),
+                pl.BlockSpec((1, share, rows), lambda i, at: (jnp.maximum(i - 1, 0), 0, 0)),
+            ),
+            scratch_shapes=[
+                pltpu.VMEM((rows, heads, width), jnp.float32),
+                pltpu.VMEM((heads, width, rows), jnp.bfloat16),
+            ],
+        ),
+        out_shape=(
+            jax.ShapeDtypeStruct((share, rows), jnp.float32),
+            jax.ShapeDtypeStruct((shards - 1, share, rows), jnp.bfloat16),
+        ),
         compiler_params=pltpu.CompilerParams(vmem_limit_bytes=VMEM_LIMIT),
         cost_estimate=pl.CostEstimate(
             flops=4 * tokens * rows * heads * width,
@@ -61,7 +97,7 @@
             transcendentals=0,
         ),
         name="indexer",
-    )(index_key, query, weight)
+    )(place, index_key, index_query, jnp.transpose(index_weight))
 
 
 def attend_kernel(
@@ -119,7 +155,8 @@
 
     start_ref[rows] = lax.fori_loop(0, rows, list_row, 0)
 
-    low_half = lax.broadcasted_iota(jnp.int32, (width, 2 * BS), 1) < BS
+    deep = width
+    low_half = lax.broadcasted_iota(jnp.int32, (deep, 2 * BS), 1) < BS
 
     for number in range(pieces):
         cache_copy(number).wait()
@@ -174,43 +211,55 @@
         base = start_ref[number * batch]
         stop = start_ref[(number + 1) * batch]
 
+        def names_of(item):
+            code = item_ref[item]
+            row = code // groups
+            part = code % groups
+            return row, [slot_ref[part * chunk + j, offset + row] for j in range(chunk)]
+
+        def scores_of(item):
+            row, names = names_of(item)
+            keys = jnp.concatenate(
+                [
+                    jnp.where(low_half, turned_ref[names[j]], turned_ref[names[j + 1]])
+                    for j in range(0, chunk, 2)
+                ],
+                axis=1,
+            )
+            return jnp.dot(
+                query_ref[row].astype(jnp.bfloat16), keys, preferred_element_type=jnp.float32
+            )
+
+        def softmax_of(scores):
+            top = jnp.max(scores, axis=1, keepdims=True)
+            weights = jnp.exp2((scores - top) * EXP_SCALE)
+            return top, jnp.sum(weights, axis=1, keepdims=True), weights.astype(jnp.bfloat16)
+
+        def numer_of(item, weights):
+            _, names = names_of(item)
+            values = jnp.concatenate([value_ref[name] for name in names], axis=0)
+            return jnp.dot(weights, values, preferred_element_type=jnp.float32)
+
+        def keep(item, top, total, numer):
+            part_ref[item - base] = numer
+            stat_ref[0, item - base] = jnp.broadcast_to(top, (heads, 128))
+            stat_ref[1, item - base] = jnp.broadcast_to(total, (heads, 128))
+
+        def item_at(index, unrolled):
+            return jnp.minimum(base + index * UNROLL + unrolled, stop - 1)
+
         def step(index, carry):
-            done = []
-            for unrolled in range(UNROLL):
-                item = jnp.minimum(base + index * UNROLL + unrolled, stop - 1)
-                code = item_ref[item]
-                row = code // groups
-                part = code % groups
-                names = [slot_ref[part * chunk + j, offset + row] for j in range(chunk)]
-                keys = jnp.concatenate(
-                    [
-                        jnp.where(low_half, turned_ref[names[j]], turned_ref[names[j + 1]])
-                        for j in range(0, chunk, 2)
-                    ],
-                    axis=1,
-                )
-                values = jnp.concatenate([value_ref[name] for name in names], axis=0)
-                scores = jnp.dot(
-                    query_ref[row].astype(jnp.bfloat16), keys, preferred_element_type=jnp.float32
-                )
-                top = jnp.max(scores, axis=1, keepdims=True)
-                weights = jnp.exp2((scores - top) * EXP_SCALE)
-                total = jnp.sum(weights, axis=1, keepdims=True)
-                numer = jnp.dot(
-                    weights.astype(jnp.bfloat16), values, preferred_element_type=jnp.float32
-                )
-                done.append((item - base, numer, top, total))
-            for item, numer, top, total in done:
-                part_ref[item] = numer
-                stat_ref[0, item] = jnp.broadcast_to(top, (heads, 128))
-                stat_ref[1, item] = jnp.broadcast_to(total, (heads, 128))
+            items = [item_at(index, u) for u in range(UNROLL)]
+            scores = [scores_of(item) for item in items]
+            soft = [softmax_of(s) for s in scores]
+            numers = [numer_of(item, s[2]) for item, s in zip(items, soft)]
+            for item, (top, total, _), numer in zip(items, soft, numers):
+                keep(item, top, total, numer)
             return carry
 
         lax.fori_loop(0, (stop - base + UNROLL - 1) // UNROLL, step, 0)
 
-        def merge_row(index, carry):
-            tops, totals = carry
-            row = number * batch + index
+        def merge_row(row):
             count = count_ref[0, offset + row]
             first = start_ref[row] - base
             places = [
@@ -238,11 +287,20 @@
                 )
                 for part in range(groups)
             )
-            out_ref[row] = merged.astype(jnp.bfloat16)
-            here = out_lane == row
-            return jnp.where(here, peak, tops), jnp.where(here, total, totals)
-
-        return lax.fori_loop(0, batch, merge_row, stats)
+            return merged.astype(jnp.bfloat16), peak, total
+
+        def merge_rows(index, carry):
+            tops, totals = carry
+            found = [number * batch + index * MERGE + u for u in range(MERGE)]
+            merged = [merge_row(row) for row in found]
+            for row, (out, peak, total) in zip(found, merged):
+                out_ref[row] = out
+                here = out_lane == row
+                tops = jnp.where(here, peak, tops)
+                totals = jnp.where(here, total, totals)
+            return tops, totals
+
+        return lax.fori_loop(0, batch // MERGE, merge_rows, stats)
 
     blank = jnp.zeros((heads, 128), jnp.float32)
     tops, totals = lax.fori_loop(0, rows // batch, attend_batch, (blank, blank))
@@ -321,8 +379,16 @@
 
     own = jnp.transpose(cache_latent)
     peer = lax.ppermute(own, "ctx", [(i, i ^ 1) for i in range(shards)])
-    partial = index_partial(index_key, index_query, index_weight)
-    index_scores = lax.psum_scatter(partial, "head", scatter_dimension=0, tiled=True)
+    head_shards = lax.axis_size("head")
+    place = lax.axis_index("head").astype(jnp.int32).reshape(1)
+    own_scores, sent = index_partial(index_key, index_query, index_weight, place, head_shards)
+    come = [
+        lax.ppermute(
+            sent[ahead - 1], "head", [(i, (i + ahead) % head_shards) for i in range(head_shards)]
+        )
+        for ahead in range(1, head_shards)
+    ]
+    index_scores = own_scores + sum(part.astype(jnp.float32) for part in come)
 
     query = jnp.transpose(query_latent, (1, 2, 0))
     cosine, sine = rope_tables(total_rows, stretch_start)

time: 221 us -> 203 us (0.919)
  the two profiles are of different devices: /device:TPU:28 before, /device:TPU:8 now
where the time goes in v1:
time: 203 us; the launch traced here: 202 us
  Pallas kernels  143 us (70%)
  waiting for transfers between devices  41.4 us (20%)
  other arithmetic  7.32 us (4%)
  starting transfers between devices  6.84 us (3%)
  local copies, waits for them, and re-layouts  2.71 us (1%)
    pallas_call x2, Pallas kernels, attend(): pl.pallas_call(functools.partial(attend_kernel, chunk, groups), out_shape...  129 us
    ppermute x3, waiting for transfers between devices, per_device(): lax.ppermute(sent[ahead - 1], 'head', [(i, (i + ahead) % head_shards) for...  41.4 us
    pallas_call x1, Pallas kernels, index_partial(): pl.pallas_call(index_kernel, grid_spec=pltpu.PrefetchScalarGridSpec(num_s...  13.3 us
    ppermute x3, starting transfers between devices, per_device(): lax.ppermute(sent[ahead - 1], 'head', [(i, (i + ahead) % head_shards) for...  4.61 us
  transfers between devices with their start and end apart: 7, of which 3 were waited for; matrix products, arithmetic and copies ran while one was open for 3% of the time, Pallas kernels for 38%

profile of v1, /device:TPU:8, one launch (start us, length us, event | category | flops | bytes accessed | tf_op | source)
XLA Modules:
  0.0 202.4 jit_solution(9330072327770422968)
XLA Ops:
  0.6 0.1 collective-permute-start.3
  0.7 0.0 copy-start.1
  0.7 13.3 %indexer.1 = (f32[1024,256]{1,0:T(8,128)}, bf16[3,1024,256]{2,1,0:T(8,128)(2,1)}) custom-call(s32[1]{0:T(128)} %bitcast.place_ref, bf16[4096,128]{1,0:T(8,128)(2,1)} %key_ref.1, bf16[256,16,128]{2,1,0:T(8,128)(2,1)} %query_ref.1, bf16[16,256]{1,0:T(8,128)(2,1)} %bitcast.57), custom_call_target="tpu_custom_call" | custom-call | flops 8589934592 | bytes 4194304 | tf_op jit(solution)/shard_map/indexer/pallas_call | solution.py:70
  14.0 0.0 copy-start
  14.0 2.5 %slice_bitcast_fusion.2 = (bf16[1024,256]{1,0:T(8,128)(2,1)}, bf16[1024,256]{1,0:T(8,128)(2,1)S(1)}, bf16[1024,256]{1,0:T(8,128)(2,1)}) fusion(bf16[3,1024,256]{2,1,0:T(8,128)(2,1)} %get-tuple-element.11), kind=kLoop, calls=%fused_computation.8 | loop fusion | bytes 3145728 | tf_op jit(solution)/shard_map/squeeze | solution.py:387
  16.6 1.6 collective-permute-start
  18.1 1.0 collective-permute-start.1
  19.2 2.0 collective-permute-start.2
  21.9 0.0 copy-done.1
  21.9 0.1 convert_reduce_fusion
  21.9 0.2 fusion
  22.1 0.7 select_reduce_fusion.slot_ref
  22.9 0.6 and_select_fusion.count_ref
  23.4 0.8 multiply_sine_fusion
  24.3 28.8 %collective-permute-done = bf16[1024,256]{1,0:T(8,128)(2,1)S(1)} collective-permute-done((bf16[1024,256]{1,0:T(8,128)(2,1)}, bf16[1024,256]{1,0:T(8,128)(2,1)S(1)}, u32[]{:S(2)}, u32[]{:S(2)}) %collective-permute-start) | collective-permute-done | bytes 524320 | tf_op jit(solution)/shard_map/ppermute | solution.py:386
  53.0 10.9 %collective-permute-done.1 = bf16[1024,256]{1,0:T(8,128)(2,1)S(1)} collective-permute-done((bf16[1024,256]{1,0:T(8,128)(2,1)}, bf16[1024,256]{1,0:T(8,128)(2,1)S(1)}, u32[]{:S(2)}, u32[]{:S(2)}) %collective-permute-start.1) | collective-permute-done | bytes 524320 | tf_op jit(solution)/shard_map/ppermute | solution.py:386
  64.0 1.7 collective-permute-done.2
  65.7 0.0 copy-done
  65.7 1.2 add_add_fusion
  66.8 0.0 collective-permute-done.3.peer_hbm
  66.8 64.6 %attend.2 = (bf16[64,32,512]{2,1,0:T(8,128)(2,1)}, f32[32,128]{1,0:T(8,128)}, f32[32,128]{1,0:T(8,128)}) custom-call(s32[1]{0:T(128)} %bitcast.5.offset_ref, s32[1,256]{1,0:T(1,128)} %and_select_fusion.count_ref, s32[24,256]{1,0:T(8,128)} %select_reduce_fusion.slot_ref, bf16[32,576,256]{2,1,0:T(8,128)(2,1)} %bitcast.52, ...), custom_call_target="tpu_custom_call" | custom-call | flops 40000000000 | bytes 16777216 | tf_op jit(solution)/shard_map/attend/pallas_call | solution.py:319
  131.5 0.1 collective-permute-start.5
  131.6 2.0 collective-permute-start.6
  133.6 0.1 collective-permute-start.4
  133.7 64.6 %attend.3 = (bf16[64,32,512]{2,1,0:T(8,128)(2,1)}, f32[32,128]{1,0:T(8,128)}, f32[32,128]{1,0:T(8,128)}) custom-call(s32[1]{0:T(128)} %bitcast.11.offset_ref, s32[1,256]{1,0:T(1,128)} %and_select_fusion.count_ref, s32[24,256]{1,0:T(8,128)} %select_reduce_fusion.slot_ref, bf16[32,576,256]{2,1,0:T(8,128)(2,1)} %bitcast.53, ...), custom_call_target="tpu_custom_call" | custom-call | flops 40000000000 | bytes 16777216 | tf_op jit(solution)/shard_map/attend/pallas_call | solution.py:319
  198.2 0.0 collective-permute-done.5
  198.2 0.0 collective-permute-done.6
  198.2 0.8 fusion.18
  199.0 0.1 copy.11
  199.1 0.1 copy.12
  199.2 0.0 collective-permute-done.4
  199.2 3.2 %add_convert_fusion = bf16[64,32,512]{2,1,0:T(8,128)(2,1)} fusion(bf16[64,32,512]{2,1,0:T(8,128)(2,1)} %get-tuple-element.17, bf16[64,32,512]{2,1,0:T(8,128)(2,1)S(1)} %collective-permute-done.4, f32[64,32]{1,0:T(8,128)S(1)} %copy.12, f32[64,32]{1,0:T(8,128)S(1)} %copy.11), kind=kLoop, calls=%fused_computation | loop fusion | flops 6291456 | bytes 6307840 | tf_op jit(solution)/shard_map/convert_element_type | solution.py:417
  (4 shorter events, 0.0 us)
Async XLA Ops:
  0.6 66.2 %collective-permute-start.3 = (bf16[576,4096]{1,0:T(8,128)(2,1)}, bf16[576,4096]{1,0:T(8,128)(2,1)}, u32[]{:S(2)}, u32[]{:S(2)}) collective-permute-start(bf16[576,4096]{1,0:T(8,128)(2,1)} %bitcast.54), channel_id=1, source_target_pairs={{0,4},{4,0},{8,12},{12,8},{1,5},{5,1},{9,13},{13,9},{2,6},{6,2},{1... | collective-permute-start | bytes 14155784 | tf_op jit(solution)/shard_map/ppermute | solution.py:381
  0.7 21.1 %copy-start.1 = (s32[256,32]{0,1:T(8,128)S(1)}, s32[256,32]{0,1:T(8,128)}, u32[]{:S(2)}) copy-start(s32[256,32]{0,1:T(8,128)} %param.12) | copy-start | bytes 98308
  14.0 51.6 %copy-start = (f32[1024,256]{1,0:T(8,128)S(1)}, f32[1024,256]{1,0:T(8,128)}, u32[]{:S(2)}) copy-start(f32[1024,256]{1,0:T(8,128)} %get-tuple-element.10) | copy-start | bytes 3145732
  16.6 36.5 %collective-permute-start = (bf16[1024,256]{1,0:T(8,128)(2,1)}, bf16[1024,256]{1,0:T(8,128)(2,1)S(1)}, u32[]{:S(2)}, u32[]{:S(2)}) collective-permute-start(bf16[1024,256]{1,0:T(8,128)(2,1)} %get-tuple-element.23), channel_id=1, source_target_pairs={{0,1},{1,2},{2,3},{3,0},{4,5},{5,6},{6,7},{7,4},{8,9},{9,10},{10,1... | collective-permute-start | bytes 1572872 | tf_op jit(solution)/shard_map/ppermute | solution.py:386
  18.1 45.8 %collective-permute-start.1 = (bf16[1024,256]{1,0:T(8,128)(2,1)}, bf16[1024,256]{1,0:T(8,128)(2,1)S(1)}, u32[]{:S(2)}, u32[]{:S(2)}) collective-permute-start(bf16[1024,256]{1,0:T(8,128)(2,1)} %get-tuple-element.25), channel_id=1, source_target_pairs={{0,2},{1,3},{2,0},{3,1},{4,6},{5,7},{6,4},{7,5},{8,10},{9,11},{10,... | collective-permute-start | bytes 1572872 | tf_op jit(solution)/shard_map/ppermute | solution.py:386
  19.2 46.5 %collective-permute-start.2 = (bf16[1024,256]{1,0:T(8,128)(2,1)S(1)}, bf16[1024,256]{1,0:T(8,128)(2,1)S(1)}, u32[]{:S(2)}, u32[]{:S(2)}) collective-permute-start(bf16[1024,256]{1,0:T(8,128)(2,1)S(1)} %get-tuple-element.24), channel_id=1, source_target_pairs={{0,3},{1,0},{2,1},{3,2},{4,7},{5,4},{6,5},{7,6},{8,11},{9,8},{10,9... | collective-permute-start | bytes 1572872 | tf_op jit(solution)/shard_map/ppermute | solution.py:386
  131.5 66.7 %collective-permute-start.5 = (f32[32,128]{1,0:T(8,128)}, f32[32,128]{1,0:T(8,128)S(1)}, u32[]{:S(2)}, u32[]{:S(2)}) collective-permute-start(f32[32,128]{1,0:T(8,128)} %get-tuple-element.13), channel_id=1, source_target_pairs={{0,8},{4,12},{8,0},{12,4},{1,9},{5,13},{9,1},{13,5},{2,10},{6,14},... | collective-permute-start | bytes 49160 | tf_op jit(solution)/shard_map/ppermute | solution.py:407
  131.6 66.7 %collective-permute-start.6 = (f32[32,128]{1,0:T(8,128)}, f32[32,128]{1,0:T(8,128)S(1)}, u32[]{:S(2)}, u32[]{:S(2)}) collective-permute-start(f32[32,128]{1,0:T(8,128)} %get-tuple-element.15), channel_id=1, source_target_pairs={{0,8},{4,12},{8,0},{12,4},{1,9},{5,13},{9,1},{13,5},{2,10},{6,14},... | collective-permute-start | bytes 49160 | tf_op jit(solution)/shard_map/ppermute | solution.py:407
  133.6 65.6 %collective-permute-start.4 = (bf16[64,32,512]{2,1,0:T(8,128)(2,1)}, bf16[64,32,512]{2,1,0:T(8,128)(2,1)S(1)}, u32[]{:S(2)}, u32[]{:S(2)}) collective-permute-start(bf16[64,32,512]{2,1,0:T(8,128)(2,1)} %get-tuple-element.12), channel_id=1, source_target_pairs={{0,8},{4,12},{8,0},{12,4},{1,9},{5,13},{9,1},{13,5},{2,10},{6,14},... | collective-permute-start | bytes 6291464 | tf_op jit(solution)/shard_map/ppermute | solution.py:407

commit v2 on v1

--- a/solution.py
+++ b/solution.py
@@ -27,8 +27,9 @@
     return jnp.cos(angle), jnp.sin(angle)
 
 
-def index_kernel(place_ref, key_ref, query_ref, weight_ref, own_ref, sent_ref, wide_ref, turned_ref):
+def index_kernel(place_ref, key_ref, query_ref, weight_ref, own_ref, *rest):
     del place_ref
+    sent_hbm, (wide_ref, turned_ref, sent_ref, sems) = rest[:-4], rest[-4:]
     heads, _, rows = turned_ref.shape
     share = key_ref.shape[0]
     step = pl.program_id(0)
@@ -60,7 +61,19 @@
     @pl.when(step > 0)
     def _():
         for first in range(0, share, count):
-            sent_ref[0, pl.ds(first, count)] = scores(first, count).astype(jnp.bfloat16)
+            sent_ref[step - 1, pl.ds(first, count)] = scores(first, count).astype(jnp.bfloat16)
+
+    copies = [
+        pltpu.make_async_copy(sent_ref.at[slot], target, sems.at[slot])
+        for slot, target in enumerate(sent_hbm)
+    ]
+    for slot, copy in enumerate(copies):
+        pl.when(step == slot + 1)(copy.start)
+
+    @pl.when(step == len(copies))
+    def _():
+        for copy in copies:
+            copy.wait()
 
 
 def index_partial(index_key, index_query, index_weight, place, shards):
@@ -79,17 +92,17 @@
             ],
             out_specs=(
                 pl.BlockSpec((share, rows), lambda i, at: (0, 0)),
-                pl.BlockSpec((1, share, rows), lambda i, at: (jnp.maximum(i - 1, 0), 0, 0)),
-            ),
+            )
+            + (pl.BlockSpec(memory_space=pl.ANY),) * (shards - 1),
             scratch_shapes=[
                 pltpu.VMEM((rows, heads, width), jnp.float32),
                 pltpu.VMEM((heads, width, rows), jnp.bfloat16),
+                pltpu.VMEM((shards - 1, share, rows), jnp.bfloat16),
+                pltpu.SemaphoreType.DMA((shards - 1,)),
             ],
         ),
-        out_shape=(
-            jax.ShapeDtypeStruct((share, rows), jnp.float32),
-            jax.ShapeDtypeStruct((shards - 1, share, rows), jnp.bfloat16),
-        ),
+        out_shape=(jax.ShapeDtypeStruct((share, rows), jnp.float32),)
+        + (jax.ShapeDtypeStruct((share, rows), jnp.bfloat16),) * (shards - 1),
         compiler_params=pltpu.CompilerParams(vmem_limit_bytes=VMEM_LIMIT),
         cost_estimate=pl.CostEstimate(
             flops=4 * tokens * rows * heads * width,
@@ -112,8 +125,7 @@
     own_hbm,
     peer_hbm,
     out_ref,
-    top_ref,
-    total_ref,
+    level_ref,
     stage_ref,
     turned_ref,
     value_ref,
@@ -304,8 +316,8 @@
 
     blank = jnp.zeros((heads, 128), jnp.float32)
     tops, totals = lax.fori_loop(0, rows // batch, attend_batch, (blank, blank))
-    top_ref[...] = tops
-    total_ref[...] = totals
+    level_ref[0] = tops
+    level_ref[1] = totals
 
 
 def attend(offset, counts, slots, query, cosine, sine, own, peer, rows, chunk, groups):
@@ -320,11 +332,10 @@
         functools.partial(attend_kernel, chunk, groups),
         out_shape=(
             jax.ShapeDtypeStruct((rows, heads, LATENT_WIDTH), jnp.bfloat16),
-            jax.ShapeDtypeStruct((heads, 128), jnp.float32),
-            jax.ShapeDtypeStruct((heads, 128), jnp.float32),
+            jax.ShapeDtypeStruct((2, heads, 128), jnp.float32),
         ),
         in_specs=[smem, smem, smem, hbm, vmem, vmem, hbm, hbm],
-        out_specs=(vmem, vmem, vmem),
+        out_specs=(vmem, vmem),
         scratch_shapes=[
             pltpu.VMEM((2, width, tokens // 2), jnp.bfloat16),
             pltpu.VMEM((2 * blocks, width, 2 * BS), jnp.bfloat16),
@@ -381,14 +392,13 @@
     peer = lax.ppermute(own, "ctx", [(i, i ^ 1) for i in range(shards)])
     head_shards = lax.axis_size("head")
     place = lax.axis_index("head").astype(jnp.int32).reshape(1)
-    own_scores, sent = index_partial(index_key, index_query, index_weight, place, head_shards)
+    own_scores, *sent = index_partial(index_key, index_query, index_weight, place, head_shards)
     come = [
         lax.ppermute(
             sent[ahead - 1], "head", [(i, (i + ahead) % head_shards) for i in range(head_shards)]
         )
         for ahead in range(1, head_shards)
     ]
-    index_scores = own_scores + sum(part.astype(jnp.float32) for part in come)
 
     query = jnp.transpose(query_latent, (1, 2, 0))
     cosine, sine = rope_tables(total_rows, stretch_start)
@@ -407,8 +417,10 @@
         parts.append([lax.ppermute(part, "ctx", moves) for part in attend_for(owner)])
     parts.append(attend_for(me))
 
-    peak = functools.reduce(jnp.maximum, [part[1] for part in parts])
-    shares = [jnp.exp2((part[1] - peak) * EXP_SCALE) * part[2] for part in parts]
+    come, parts[-1] = lax.optimization_barrier((come, parts[-1]))
+    index_scores = own_scores + sum(part.astype(jnp.float32) for part in come)
+    peak = functools.reduce(jnp.maximum, [part[1][0] for part in parts])
+    shares = [jnp.exp2((part[1][0] - peak) * EXP_SCALE) * part[1][1] for part in parts]
     whole = sum(shares)
     attended = sum(
         part[0].astype(jnp.float32) * jnp.transpose((share / whole)[:, :rows])[:, :, None]

time: 203 us -> 150 us (0.74)
  the two profiles are of different devices: /device:TPU:8 before, /device:TPU:3 now
where the time goes in v2:
time: 150 us; the launch traced here: 151 us
  Pallas kernels  101 us (67%)
  starting transfers between devices  40.3 us (27%)
  other arithmetic  8.34 us (6%)
    pallas_call x2, Pallas kernels, attend(): pl.pallas_call(functools.partial(attend_kernel, chunk, groups), out_shape...  86.6 us
    ppermute x2, starting transfers between devices, per_device(): lax.ppermute(part, 'ctx', moves)  34.8 us
    pallas_call x1, Pallas kernels, index_partial(): pl.pallas_call(index_kernel, grid_spec=pltpu.PrefetchScalarGridSpec(num_s...  14 us
    ppermute x3, starting transfers between devices, per_device(): lax.ppermute(sent[ahead - 1], 'head', [(i, (i + ahead) % head_shards) for...  4.72 us
    convert_element_type x1, other arithmetic, per_device(): return (index_scores, attended.astype(jnp.bfloat16))  3.18 us
  transfers between devices with their start and end apart: 6, of which 0 were waited for; matrix products, arithmetic and copies ran while one was open for 4% of the time, Pallas kernels for 67%

profile of v2, /device:TPU:3, one launch (start us, length us, event | category | flops | bytes accessed | tf_op | source)
XLA Modules:
  0.0 151.0 jit_solution(16277521421237735287)
XLA Ops:
  0.6 0.7 collective-permute-start.3
  1.4 0.0 copy-start.1
  1.4 14.0 %indexer.1 = (f32[1024,256]{1,0:T(8,128)}, bf16[1024,256]{1,0:T(8,128)(2,1)}, bf16[1024,256]{1,0:T(8,128)(2,1)}, bf16[1024,256]{1,0:T(8,128)(2,1)}) custom-call(s32[1]{0:T(128)} %bitcast.place_ref, bf16[4096,128]{1,0:T(8,128)(2,1)} %key_ref.1, bf16[256,16,128]{2,1,0:T(8,128)(2,1)} %query_ref.1, bf16[16,256]{1,0:T(8,128)(2,1)} %bitcast.72), custom_call_target="tpu_custom_call" | custom-call | flops 8589934592 | bytes 4194304 | tf_op jit(solution)/shard_map/indexer/pallas_call | solution.py:83
  15.3 1.3 collective-permute-start
  16.7 2.3 %collective-permute-start.1 = (bf16[1024,256]{1,0:T(8,128)(2,1)}, bf16[1024,256]{1,0:T(8,128)(2,1)S(1)}, u32[]{:S(2)}, u32[]{:S(2)}) collective-permute-start(bf16[1024,256]{1,0:T(8,128)(2,1)} %get-tuple-element.17), channel_id=1, source_target_pairs={{0,2},{1,3},{2,0},{3,1},{4,6},{5,7},{6,4},{7,5},{8,10},{9,11},{10,... | collective-permute-start | bytes 1572872 | tf_op jit(solution)/shard_map/ppermute | solution.py:397
  19.0 1.1 collective-permute-start.2
  20.8 0.0 copy-done.1
  20.8 0.1 convert_reduce_fusion
  20.8 0.2 fusion
  21.0 0.7 select_reduce_fusion.slot_ref
  21.8 0.5 and_select_fusion.count_ref
  22.3 0.8 multiply_sine_fusion
  23.1 0.0 collective-permute-done.3.peer_hbm
  23.1 42.3 %attend.3 = (bf16[64,32,512]{2,1,0:T(8,128)(2,1)}, f32[2,32,128]{2,1,0:T(8,128)}) custom-call(s32[1]{0:T(128)} %bitcast.8.offset_ref, s32[1,256]{1,0:T(1,128)} %and_select_fusion.count_ref, s32[24,256]{1,0:T(8,128)} %select_reduce_fusion.slot_ref, bf16[32,576,256]{2,1,0:T(8,128)(2,1)} %bitcast.67, f32[32,256]{1,0:T(8,128)} %get-tuple-element.37.cosine_ref, ...), custom_call_target="tpu_custom_call" | custom-call | flops 40000000000 | bytes 16777216 | tf_op jit(solution)/shard_map/attend/pallas_call | solution.py:331
  65.5 18.0 %collective-permute-start.4 = (bf16[64,32,512]{2,1,0:T(8,128)(2,1)}, bf16[64,32,512]{2,1,0:T(8,128)(2,1)S(1)}, u32[]{:S(2)}, u32[]{:S(2)}) collective-permute-start(bf16[64,32,512]{2,1,0:T(8,128)(2,1)} %get-tuple-element.24), channel_id=1, source_target_pairs={{0,8},{4,12},{8,0},{12,4},{1,9},{5,13},{9,1},{13,5},{2,10},{6,14},... | collective-permute-start | bytes 6291464 | tf_op jit(solution)/shard_map/ppermute | solution.py:417
  83.5 0.0 copy-start.2
  83.5 0.0 copy-start
  83.5 44.3 %attend.2 = (bf16[64,32,512]{2,1,0:T(8,128)(2,1)}, f32[2,32,128]{2,1,0:T(8,128)}) custom-call(s32[1]{0:T(128)} %bitcast.2.offset_ref, s32[1,256]{1,0:T(1,128)} %and_select_fusion.count_ref, s32[24,256]{1,0:T(8,128)} %select_reduce_fusion.slot_ref, bf16[32,576,256]{2,1,0:T(8,128)(2,1)} %bitcast.68, f32[32,256]{1,0:T(8,128)} %get-tuple-element.37.cosine_ref, ...), custom_call_target="tpu_custom_call" | custom-call | flops 40000000000 | bytes 16777216 | tf_op jit(solution)/shard_map/attend/pallas_call | solution.py:331
  127.8 0.0 collective-permute-done
  127.8 0.0 collective-permute-done.1
  127.8 0.0 collective-permute-done.2
  127.8 0.0 copy-done.2
  127.8 16.8 %collective-permute-start.5 = (f32[2,32,128]{2,1,0:T(8,128)S(1)}, f32[2,32,128]{2,1,0:T(8,128)S(1)}, u32[]{:S(2)}, u32[]{:S(2)}) collective-permute-start(f32[2,32,128]{2,1,0:T(8,128)S(1)} %copy-done.2), channel_id=1, source_target_pairs={{0,8},{4,12},{8,0},{12,4},{1,9},{5,13},{9,1},{13,5},{2,10},{6,14},... | collective-permute-start | bytes 98312 | tf_op jit(solution)/shard_map/ppermute | solution.py:417
  144.6 0.0 copy-done
  144.6 2.2 %add_add_fusion = f32[1024,256]{1,0:T(8,128)} fusion(f32[1024,256]{1,0:T(8,128)S(1)} %copy-done, bf16[1024,256]{1,0:T(8,128)(2,1)} %collective-permute-done.2, bf16[1024,256]{1,0:T(8,128)(2,1)S(1)} %collective-permute-done.1, bf16[1024,256]{1,0:T(8,128)(2,1)S(1)} %collective-permute-done), kind=kLoop, calls=%fused_computation.3 | loop fusion | flops 1572864 | bytes 3670016 | tf_op jit(solution)/shard_map/add | solution.py:421
  146.8 0.0 collective-permute-done.5
  146.8 0.8 fusion.18
  147.6 0.1 copy.12
  147.7 0.1 copy.11
  147.8 0.0 collective-permute-done.4
  147.8 3.2 %add_convert_fusion = bf16[64,32,512]{2,1,0:T(8,128)(2,1)} fusion(bf16[64,32,512]{2,1,0:T(8,128)(2,1)} %get-tuple-element.27, bf16[64,32,512]{2,1,0:T(8,128)(2,1)S(1)} %collective-permute-done.4, f32[64,32]{1,0:T(8,128)S(1)} %copy.12, f32[64,32]{1,0:T(8,128)S(1)} %copy.11), kind=kLoop, calls=%fused_computation | loop fusion | flops 6291456 | bytes 6307840 | tf_op jit(solution)/shard_map/convert_element_type | solution.py:429
  (4 shorter events, 0.0 us)
Async XLA Ops:
  0.6 22.5 %collective-permute-start.3 = (bf16[576,4096]{1,0:T(8,128)(2,1)}, bf16[576,4096]{1,0:T(8,128)(2,1)}, u32[]{:S(2)}, u32[]{:S(2)}) collective-permute-start(bf16[576,4096]{1,0:T(8,128)(2,1)} %bitcast.69), channel_id=1, source_target_pairs={{0,4},{4,0},{8,12},{12,8},{1,5},{5,1},{9,13},{13,9},{2,6},{6,2},{1... | collective-permute-start | bytes 14155784 | tf_op jit(solution)/shard_map/ppermute | solution.py:392
  1.4 19.4 %copy-start.1 = (s32[256,32]{0,1:T(8,128)S(1)}, s32[256,32]{0,1:T(8,128)}, u32[]{:S(2)}) copy-start(s32[256,32]{0,1:T(8,128)} %param.12) | copy-start | bytes 98308
  15.3 112.4 %collective-permute-start = (bf16[1024,256]{1,0:T(8,128)(2,1)}, bf16[1024,256]{1,0:T(8,128)(2,1)S(1)}, u32[]{:S(2)}, u32[]{:S(2)}) collective-permute-start(bf16[1024,256]{1,0:T(8,128)(2,1)} %get-tuple-element.16), channel_id=1, source_target_pairs={{0,1},{1,2},{2,3},{3,0},{4,5},{5,6},{6,7},{7,4},{8,9},{9,10},{10,1... | collective-permute-start | bytes 1572872 | tf_op jit(solution)/shard_map/ppermute | solution.py:397
  16.7 111.1 %collective-permute-start.1 = (bf16[1024,256]{1,0:T(8,128)(2,1)}, bf16[1024,256]{1,0:T(8,128)(2,1)S(1)}, u32[]{:S(2)}, u32[]{:S(2)}) collective-permute-start(bf16[1024,256]{1,0:T(8,128)(2,1)} %get-tuple-element.17), channel_id=1, source_target_pairs={{0,2},{1,3},{2,0},{3,1},{4,6},{5,7},{6,4},{7,5},{8,10},{9,11},{10,... | collective-permute-start | bytes 1572872 | tf_op jit(solution)/shard_map/ppermute | solution.py:397
  19.0 108.8 %collective-permute-start.2 = (bf16[1024,256]{1,0:T(8,128)(2,1)}, bf16[1024,256]{1,0:T(8,128)(2,1)}, u32[]{:S(2)}, u32[]{:S(2)}) collective-permute-start(bf16[1024,256]{1,0:T(8,128)(2,1)} %get-tuple-element.18), channel_id=1, source_target_pairs={{0,3},{1,0},{2,1},{3,2},{4,7},{5,4},{6,5},{7,6},{8,11},{9,8},{10,9... | collective-permute-start | bytes 1572872 | tf_op jit(solution)/shard_map/ppermute | solution.py:397
  65.5 82.3 %collective-permute-start.4 = (bf16[64,32,512]{2,1,0:T(8,128)(2,1)}, bf16[64,32,512]{2,1,0:T(8,128)(2,1)S(1)}, u32[]{:S(2)}, u32[]{:S(2)}) collective-permute-start(bf16[64,32,512]{2,1,0:T(8,128)(2,1)} %get-tuple-element.24), channel_id=1, source_target_pairs={{0,8},{4,12},{8,0},{12,4},{1,9},{5,13},{9,1},{13,5},{2,10},{6,14},... | collective-permute-start | bytes 6291464 | tf_op jit(solution)/shard_map/ppermute | solution.py:417
  83.5 44.3 %copy-start.2 = (f32[2,32,128]{2,1,0:T(8,128)S(1)}, f32[2,32,128]{2,1,0:T(8,128)}, u32[]{:S(2)}) copy-start(f32[2,32,128]{2,1,0:T(8,128)} %get-tuple-element.25) | copy-start | bytes 98308
  83.5 61.1 %copy-start = (f32[1024,256]{1,0:T(8,128)S(1)}, f32[1024,256]{1,0:T(8,128)}, u32[]{:S(2)}) copy-start(f32[1024,256]{1,0:T(8,128)} %get-tuple-element.15) | copy-start | bytes 3145732
  127.8 19.0 %collective-permute-start.5 = (f32[2,32,128]{2,1,0:T(8,128)S(1)}, f32[2,32,128]{2,1,0:T(8,128)S(1)}, u32[]{:S(2)}, u32[]{:S(2)}) collective-permute-start(f32[2,32,128]{2,1,0:T(8,128)S(1)} %copy-done.2), channel_id=1, source_target_pairs={{0,8},{4,12},{8,0},{12,4},{1,9},{5,13},{9,1},{13,5},{2,10},{6,14},... | collective-permute-start | bytes 98312 | tf_op jit(solution)/shard_map/ppermute | solution.py:417

commit v3 on v2

--- a/solution.py
+++ b/solution.py
@@ -16,6 +16,7 @@
 EXP_SCALE = QKD**-0.5 * 1.4426950408889634
 UNROLL = 8
 MERGE = 4
+MOVE_COST = 44
 VMEM_LIMIT = 58 * 2**20
 
 
@@ -113,41 +114,22 @@
     )(place, index_key, index_query, jnp.transpose(index_weight))
 
 
-def attend_kernel(
-    chunk,
-    groups,
-    offset_ref,
-    count_ref,
-    slot_ref,
-    query_hbm,
-    cosine_ref,
-    sine_ref,
-    own_hbm,
-    peer_hbm,
-    out_ref,
-    level_ref,
-    stage_ref,
-    turned_ref,
-    value_ref,
-    raw_ref,
-    query_ref,
-    part_ref,
-    stat_ref,
-    item_ref,
-    start_ref,
-    sems,
-):
+def attend_kernel(chunk, groups, sources, *refs):
+    offset_ref, count_ref, slot_ref, query_hbm, cosine_ref, sine_ref = refs[:6]
+    cache_hbm, refs = refs[6 : 6 + sources], refs[6 + sources :]
+    out_ref, level_ref, stage_ref, turned_ref, value_ref, raw_ref, query_ref = refs[:7]
+    part_ref, stat_ref, item_ref, start_ref, sems = refs[7:]
     rows, heads, width = query_ref.shape
-    tokens = own_hbm.shape[1]
+    tokens = cache_hbm[0].shape[1]
     half = DR // 2
     piece = stage_ref.shape[2]
-    pieces = 2 * tokens // piece
+    pieces = sources * tokens // piece
     offset = offset_ref[0]
     tile = pl.multiple_of(offset // 128 * 128, 128)
     inside = offset - tile
 
     def cache_copy(number):
-        source = own_hbm if number * piece < tokens else peer_hbm
+        source = cache_hbm[number * piece // tokens]
         return pltpu.make_async_copy(
             source.at[:, pl.ds(number * piece % tokens, piece)],
             stage_ref.at[number % 2],
@@ -165,7 +147,8 @@
             item_ref[filled + part] = row * groups + part
         return filled + count_ref[0, offset + row]
 
-    start_ref[rows] = lax.fori_loop(0, rows, list_row, 0)
+    found = lax.fori_loop(0, rows, list_row, 0)
+    start_ref[rows] = found
 
     deep = width
     low_half = lax.broadcasted_iota(jnp.int32, (deep, 2 * BS), 1) < BS
@@ -184,7 +167,7 @@
             value_ref[block + 1] = values[BS:]
             return carry
 
-        lax.fori_loop(0, piece // 128, turn, 0)
+        lax.fori_loop(0, jnp.where(found > 0, piece // 128, 0), turn, 0)
         if number + 2 < pieces:
             cache_copy(number + 2).start()
 
@@ -213,7 +196,7 @@
             query_ref[:, block * 8 + head, :] = picked
         return carry
 
-    lax.fori_loop(0, heads // 8, turn_query, 0)
+    lax.fori_loop(0, jnp.where(found > 0, heads // 8, 0), turn_query, 0)
 
     out_lane = lax.broadcasted_iota(jnp.int32, (heads, 128), 1)
     wide = LATENT_WIDTH // 128
@@ -320,26 +303,28 @@
     level_ref[1] = totals
 
 
-def attend(offset, counts, slots, query, cosine, sine, own, peer, rows, chunk, groups):
+def attend(offset, counts, slots, query, cosine, sine, caches, rows, chunk, groups, work):
     heads, width = query.shape[0], query.shape[1]
-    tokens = own.shape[1]
-    blocks = tokens // BS
+    tokens = caches[0].shape[1]
+    sources = len(caches)
+    blocks = sources * tokens // BS
+    piece = min(tokens, 2048)
     smem = pl.BlockSpec(memory_space=pltpu.SMEM)
     vmem = pl.BlockSpec(memory_space=pltpu.VMEM)
     hbm = pl.BlockSpec(memory_space=pl.ANY)
     batch = min(rows, 32)
     return pl.pallas_call(
-        functools.partial(attend_kernel, chunk, groups),
+        functools.partial(attend_kernel, chunk, groups, sources),
         out_shape=(
             jax.ShapeDtypeStruct((rows, heads, LATENT_WIDTH), jnp.bfloat16),
             jax.ShapeDtypeStruct((2, heads, 128), jnp.float32),
         ),
-        in_specs=[smem, smem, smem, hbm, vmem, vmem, hbm, hbm],
+        in_specs=[smem, smem, smem, hbm, vmem, vmem] + [hbm] * sources,
         out_specs=(vmem, vmem),
         scratch_shapes=[
-            pltpu.VMEM((2, width, tokens // 2), jnp.bfloat16),
-            pltpu.VMEM((2 * blocks, width, 2 * BS), jnp.bfloat16),
-            pltpu.VMEM((2 * blocks, BS, LATENT_WIDTH), jnp.bfloat16),
+            pltpu.VMEM((2, width, piece), jnp.bfloat16),
+            pltpu.VMEM((blocks, width, 2 * BS), jnp.bfloat16),
+            pltpu.VMEM((blocks, BS, LATENT_WIDTH), jnp.bfloat16),
             pltpu.VMEM((heads, width, 128), jnp.bfloat16),
             pltpu.VMEM((rows, heads, width), jnp.float32),
             pltpu.VMEM((batch * groups, heads, LATENT_WIDTH), jnp.float32),
@@ -350,19 +335,14 @@
         ],
         compiler_params=pltpu.CompilerParams(vmem_limit_bytes=VMEM_LIMIT),
         cost_estimate=pl.CostEstimate(
-            flops=40 * 10**9, bytes_accessed=16 * 2**20, transcendentals=2 * 10**6
+            flops=work, bytes_accessed=10**5, transcendentals=0
         ),
         name="attend",
-    )(offset, counts, slots, query, cosine, sine, own, peer)
-
-
-def chip_slots(block_ids, own_segment, peer_segment, blocks, chunk, groups):
-    ids = jnp.transpose(block_ids)
-    segment = ids // blocks
-    local = ids % blocks
-    place_of = jnp.where(segment == peer_segment, local + blocks, local)
-    owned = (segment == own_segment) | (segment == peer_segment)
-    count = ids.shape[0]
+    )(offset, counts, slots, query, cosine, sine, *caches)
+
+
+def make_slots(owned, place_of, chunk, groups):
+    count = owned.shape[0]
     before = jnp.tril(jnp.ones((count, count), jnp.float32), -1)
     place = jnp.dot(before, owned.astype(jnp.float32)).astype(jnp.int32)
     place = jnp.where(owned, place, -1)
@@ -372,6 +352,30 @@
     )
     counts = jnp.sum(owned.astype(jnp.int32), axis=0, keepdims=True) // chunk
     return counts, slots
+
+
+def plan_moves(segment, chunk, rows):
+    numbers = jnp.arange(4, dtype=jnp.int32)
+    hits = (segment[None] == numbers[:, None, None]).astype(jnp.int32)
+    count = jnp.sum(hits, axis=1) // chunk
+    owner = jnp.arange(segment.shape[1], dtype=jnp.int32) // rows
+    core, pair = owner % 2, owner // 2
+    lead = jnp.sum(count[2:], axis=0) - jnp.sum(count[:2], axis=0)
+    leads = [jnp.sum(jnp.where(core == c, lead, 0)) for c in range(2)]
+    heavy = (leads[0] + leads[1] > 0).astype(jnp.int32)
+    sign = 2 * heavy - 1
+    whole = jnp.sum(count, axis=1)
+    hot = [2 * y + (whole[2 * y + 1] > whole[2 * y]).astype(jnp.int32) for y in range(2)]
+    hot_heavy = jnp.where(heavy == 1, hot[1], hot[0])
+    excess = jnp.where(core == 0, leads[0], leads[1]) * sign - MOVE_COST
+    can = jnp.where(
+        pair != heavy, jnp.sum(jnp.where(numbers[:, None] == hot_heavy, count, 0), axis=0), 0
+    )
+    index = jnp.arange(segment.shape[1], dtype=jnp.int32)
+    earlier = (index[:, None] < index[None, :]) & (owner[:, None] == owner[None, :])
+    before = jnp.sum(jnp.where(earlier, can[:, None], 0), axis=0)
+    moved = (pair != heavy) & (2 * before < excess)
+    return hot, hot_heavy, moved
 
 
 def per_device(
@@ -389,7 +393,8 @@
     blocks = cache_latent.shape[0] // BS
 
     own = jnp.transpose(cache_latent)
-    peer = lax.ppermute(own, "ctx", [(i, i ^ 1) for i in range(shards)])
+    swap = [(i, i ^ 1) for i in range(shards)]
+    peer = lax.ppermute(own, "ctx", swap)
     head_shards = lax.axis_size("head")
     place = lax.axis_index("head").astype(jnp.int32).reshape(1)
     own_scores, *sent = index_partial(index_key, index_query, index_weight, place, head_shards)
@@ -399,23 +404,61 @@
         )
         for ahead in range(1, head_shards)
     ]
-
     query = jnp.transpose(query_latent, (1, 2, 0))
     cosine, sine = rope_tables(total_rows, stretch_start)
-    counts, slots = chip_slots(block_ids, me, me ^ 1, blocks, chunk, groups)
-
-    def attend_for(owner):
+    ids = jnp.transpose(block_ids)
+    segment = ids // blocks
+    local = ids % blocks
+    place_of = jnp.where(segment == (me ^ 1), local + blocks, local)
+    owned = segment // 2 == pair
+    share_hot = pairs == 2
+    if share_hot:
+        hot, hot_heavy, moved = plan_moves(segment, chunk, rows)
+        owned &= ~(moved[None, :] & (segment == hot_heavy))
+        my_hot = jnp.where(pair == 1, hot[1], hot[0])
+        quarter = own.shape[1] // 4
+        near = []
+        for number in range(2):
+            at = (2 * core + number) * quarter
+            sent_piece = jnp.where(
+                my_hot == me,
+                lax.dynamic_slice_in_dim(own, at, quarter, 1),
+                lax.dynamic_slice_in_dim(peer, at, quarter, 1),
+            )
+            near.append(lax.ppermute(sent_piece, "ctx", [(i, i ^ 2) for i in range(shards)]))
+        moved_place = jnp.where(
+            local // (blocks // 2) == core, local % (blocks // 2), local % (blocks // 2) + blocks // 2
+        )
+        more_counts, more_slots = make_slots(
+            moved[None, :] & (segment == hot_heavy), moved_place, chunk, groups
+        )
+    counts, slots = make_slots(owned, place_of, chunk, groups)
+
+    if share_hot:
+        counts, own_scores = lax.optimization_barrier((counts, own_scores))
+
+    def attend_for(owner, work, counts, slots, *caches):
         offset = (owner * rows).astype(jnp.int32).reshape(1)
         return attend(
-            offset, counts, slots, query, cosine, sine, own, peer, rows, chunk, groups
+            offset, counts, slots, query, cosine, sine, caches, rows, chunk, groups, work
         )
 
     parts = []
     for ahead in range(1, pairs):
         owner = ((pair + ahead) % pairs) * 2 + core
         moves = [(i, ((i // 2 + ahead) % pairs) * 2 + i % 2) for i in range(shards)]
-        parts.append([lax.ppermute(part, "ctx", moves) for part in attend_for(owner)])
-    parts.append(attend_for(me))
+        result = attend_for(owner, 40 * 10**9, counts, slots, own, peer)
+        counts, result, come = lax.optimization_barrier((counts, result, come))
+        parts.append([lax.ppermute(part, "ctx", moves) for part in result])
+    mine = attend_for(me, 10**7, counts, slots, own, peer)
+    if share_hot:
+        near, mine, parts[0][1] = lax.optimization_barrier((near, mine, parts[0][1]))
+        far = [lax.ppermute(piece, "ctx", swap) for piece in near]
+    parts.append(mine)
+
+    if share_hot:
+        more_counts, parts = lax.optimization_barrier((more_counts, parts))
+        parts.append(attend_for(me, 10**7, more_counts, more_slots, *near, *far))
 
     come, parts[-1] = lax.optimization_barrier((come, parts[-1]))
     index_scores = own_scores + sum(part.astype(jnp.float32) for part in come)

time: 150 us -> 188 us (1.25)
  the two profiles are of different devices: /device:TPU:3 before, /device:TPU:0 now
where the time goes in v3:
time: 188 us; the launch traced here: 189 us
  Pallas kernels  129 us (69%)
  other arithmetic  18.3 us (10%)
  starting transfers between devices  16.8 us (9%)
  waiting for transfers between devices  15.3 us (8%)
  between operations  5.3 us (3%)
  local copies, waits for them, and re-layouts  3.52 us (2%)
    pallas_call x3, Pallas kernels, attend(): pl.pallas_call(functools.partial(attend_kernel, chunk, groups, sources),...  115 us
    pallas_call x1, Pallas kernels, index_partial(): pl.pallas_call(index_kernel, grid_spec=pltpu.PrefetchScalarGridSpec(num_s...  13.9 us
    ppermute x2, waiting for transfers between devices, per_device(): parts.append([lax.ppermute(part, 'ctx', moves) for part in result])  12.8 us
    ppermute x2, starting transfers between devices, per_device(): parts.append([lax.ppermute(part, 'ctx', moves) for part in result])  7.13 us
    ppermute x3, starting transfers between devices, per_device(): lax.ppermute(sent[ahead - 1], 'head', [(i, (i + ahead) % head_shards) for...  6.6 us
    select_n x1, other arithmetic, per_device(): jnp.where(my_hot == me, lax.dynamic_slice_in_dim(own, at, quarter, 1), la...  4.99 us
  transfers between devices with their start and end apart: 10, of which 3 were waited for; matrix products, arithmetic and copies ran while one was open for 6% of the time, Pallas kernels for 47%

profile of v3, /device:TPU:0, one launch (start us, length us, event | category | flops | bytes accessed | tf_op | source)
XLA Modules:
  0.0 188.8 jit_solution(1538693552006406930)
XLA Ops:
  0.6 0.5 collective-permute-start
  1.2 13.9 %indexer.1 = (f32[1024,256]{1,0:T(8,128)}, bf16[1024,256]{1,0:T(8,128)(2,1)}, bf16[1024,256]{1,0:T(8,128)(2,1)}, bf16[1024,256]{1,0:T(8,128)(2,1)}) custom-call(s32[1]{0:T(128)} %bitcast.4.place_ref, bf16[4096,128]{1,0:T(8,128)(2,1)} %key_ref.1, bf16[256,16,128]{2,1,0:T(8,128)(2,1)} %query_ref.1, bf16[16,256]{1,0:T(8,128)(2,1)} %bitcast.104), custom_call_target="tpu_custom_call" | custom-call | flops 8589934592 | bytes 4194304 | tf_op jit(solution)/shard_map/indexer/pallas_call | solution.py:84
  15.1 2.7 %collective-permute-start.1 = (bf16[1024,256]{1,0:T(8,128)(2,1)}, bf16[1024,256]{1,0:T(8,128)(2,1)S(1)}, u32[]{:S(2)}, u32[]{:S(2)}) collective-permute-start(bf16[1024,256]{1,0:T(8,128)(2,1)} %get-tuple-element.40), channel_id=1, source_target_pairs={{0,1},{1,2},{2,3},{3,0},{4,5},{5,6},{6,7},{7,4},{8,9},{9,10},{10,1... | collective-permute-start | bytes 1572872 | tf_op jit(solution)/shard_map/ppermute | solution.py:402
  17.8 2.6 %collective-permute-start.2 = (bf16[1024,256]{1,0:T(8,128)(2,1)}, bf16[1024,256]{1,0:T(8,128)(2,1)S(1)}, u32[]{:S(2)}, u32[]{:S(2)}) collective-permute-start(bf16[1024,256]{1,0:T(8,128)(2,1)} %get-tuple-element.41), channel_id=1, source_target_pairs={{0,2},{1,3},{2,0},{3,1},{4,6},{5,7},{6,4},{7,5},{8,10},{9,11},{10,... | collective-permute-start | bytes 1572872 | tf_op jit(solution)/shard_map/ppermute | solution.py:402
  20.3 1.3 collective-permute-start.3
  21.7 0.1 add_select_fusion.3
  21.8 0.1 fusion.37
  21.9 0.7 fusion.31
  24.6 0.7 fusion.38
  27.8 0.1 select_reduce_fusion.3
  27.9 0.1 select_reduce_fusion.2
  28.0 1.3 compare_and_fusion.1
  29.4 0.6 and_select_fusion.1.refs_1_
  30.0 0.2 fusion.1
  30.2 0.7 select_reduce_fusion.1.refs_2_
  31.0 0.8 multiply_sine_fusion
  31.8 0.0 collective-permute-done.refs_7_
  31.8 5.0 %bitcast_select_fusion = (bf16[576,1024]{1,0:T(8,128)(2,1)}, bf16[576,1024]{1,0:T(8,128)(2,1)}) fusion(bf16[576,4096]{1,0:T(8,128)(2,1)} %collective-permute-done.refs_7_, s32[]{:T(128)S(6)} %select_n.229, bf16[4096,576]{0,1:T(8,128)(2,1)} %param.7, pred[]{:T(512)S(6)} %eq.143, s32[]{:T(128)S(6)} %select_n.227), kind=kLoop, calls=%fused_computation.1 | loop fusion | flops 1179648 | bytes 7077897 | tf_op jit(solution)/shard_map/jit(_where)/select_n | solution.py:423
  36.8 1.5 collective-permute-start.6
  38.3 0.5 collective-permute-start.5
  38.8 36.9 %attend.3 = (bf16[64,32,512]{2,1,0:T(8,128)(2,1)}, f32[2,32,128]{2,1,0:T(8,128)}) custom-call(s32[1]{0:T(128)} %bitcast.6.refs_0_, s32[1,256]{1,0:T(1,128)} %and_select_fusion.1.refs_1_, s32[24,256]{1,0:T(8,128)} %select_reduce_fusion.1.refs_2_, bf16[32,576,256]{2,1,0:T(8,128)(2,1)} %bitcast.96, f32[32,256]{1,0:T(8,128)} %get-tuple-element.91.refs_4_, ...), custom_call_target="tpu_custom_call" | custom-call | flops 40000000000 | bytes 100000 | tf_op jit(solution)/shard_map/attend/pallas_call | solution.py:316
  75.7 0.0 collective-permute-done.1
  75.8 0.8 copy-done.4
  76.5 0.1 copy-done.5
  76.7 0.2 copy-done.6
  76.9 7.1 %collective-permute-start.4 = (bf16[64,32,512]{2,1,0:T(8,128)(2,1)}, bf16[64,32,512]{2,1,0:T(8,128)(2,1)S(1)}, u32[]{:S(2)}, u32[]{:S(2)}) collective-permute-start(bf16[64,32,512]{2,1,0:T(8,128)(2,1)} %get-tuple-element.46), channel_id=1, source_target_pairs={{0,8},{4,12},{8,0},{12,4},{1,9},{5,13},{9,1},{13,5},{2,10},{6,14},... | collective-permute-start | bytes 6291464 | tf_op jit(solution)/shard_map/ppermute | solution.py:452
  84.0 0.0 collective-permute-start.7
  84.0 38.6 %attend.4 = (bf16[64,32,512]{2,1,0:T(8,128)(2,1)}, f32[2,32,128]{2,1,0:T(8,128)}) custom-call(s32[1]{0:T(128)} %bitcast.10.refs_0_, s32[1,256]{1,0:T(1,128)} %and_select_fusion.1.refs_1_, s32[24,256]{1,0:T(8,128)} %select_reduce_fusion.1.refs_2_, bf16[32,576,256]{2,1,0:T(8,128)(2,1)} %bitcast.97, f32[32,256]{1,0:T(8,128)} %get-tuple-element.91.refs_4_, ...), custom_call_target="tpu_custom_call" | custom-call | flops 10000000 | bytes 100000 | tf_op jit(solution)/shard_map/attend/pallas_call | solution.py:316
  122.7 12.8 %collective-permute-done.7 = f32[2,32,128]{2,1,0:T(8,128)S(1)} collective-permute-done((f32[2,32,128]{2,1,0:T(8,128)}, f32[2,32,128]{2,1,0:T(8,128)S(1)}, u32[]{:S(2)}, u32[]{:S(2)}) %collective-permute-start.7) | collective-permute-done | bytes 32800 | tf_op jit(solution)/shard_map/ppermute | solution.py:452
  135.4 0.0 collective-permute-done.6.refs_7_
  135.4 0.0 collective-permute-done.5.refs_6_
  135.4 0.1 collective-permute-start.8
  135.5 0.5 collective-permute-start.9
  136.0 0.2 fusion
  136.2 0.7 select_reduce_fusion.refs_2_
  136.9 0.6 and_select_fusion.refs_1_
  137.5 2.0 %collective-permute-done.8.refs_8_ = bf16[576,1024]{1,0:T(8,128)(2,1)S(1)} collective-permute-done((bf16[576,1024]{1,0:T(8,128)(2,1)}, bf16[576,1024]{1,0:T(8,128)(2,1)S(1)}, u32[]{:S(2)}, u32[]{:S(2)}) %collective-permute-start.8) | collective-permute-done | bytes 1179680 | tf_op jit(solution)/shard_map/ppermute | solution.py:456
  139.4 0.6 collective-permute-done.9.refs_9_
  140.0 0.5 copy-done.2
  140.5 1.0 copy-done.3
  141.5 39.6 %attend.5 = (bf16[64,32,512]{2,1,0:T(8,128)(2,1)}, f32[2,32,128]{2,1,0:T(8,128)}) custom-call(s32[1]{0:T(128)} %bitcast.10.refs_0_, s32[1,256]{1,0:T(1,128)} %and_select_fusion.refs_1_, s32[24,256]{1,0:T(8,128)} %select_reduce_fusion.refs_2_, bf16[32,576,256]{2,1,0:T(8,128)(2,1)} %bitcast.98, f32[32,256]{1,0:T(8,128)} %get-tuple-element.91.refs_4_, ...), custom_call_target="tpu_custom_call" | custom-call | flops 10000000 | bytes 100000 | tf_op jit(solution)/shard_map/attend/pallas_call | solution.py:316
  181.2 0.8 add_add_fusion.1
  182.0 0.1 copy.12
  182.0 0.1 copy.13
  182.1 0.1 copy.14
  182.2 0.0 copy-start
  182.2 3.0 %add_add_fusion = f32[1024,256]{1,0:T(8,128)} fusion(f32[1024,256]{1,0:T(8,128)} %get-tuple-element.36, bf16[1024,256]{1,0:T(8,128)(2,1)} %copy-done.6, bf16[1024,256]{1,0:T(8,128)(2,1)} %copy-done.5, bf16[1024,256]{1,0:T(8,128)(2,1)} %copy-done.4), kind=kLoop, calls=%fused_computation.7 | loop fusion | flops 1572864 | bytes 3670016 | tf_op jit(solution)/shard_map/add | solution.py:464
  185.2 3.5 %add_convert_fusion = bf16[64,32,512]{2,1,0:T(8,128)(2,1)} fusion(bf16[64,32,512]{2,1,0:T(8,128)(2,1)} %get-tuple-element.67, bf16[64,32,512]{2,1,0:T(8,128)(2,1)S(1)} %copy-done, bf16[64,32,512]{2,1,0:T(8,128)(2,1)S(1)} %collective-permute-done.4, f32[64,32]{1,0:T(8,128)S(1)} %copy.14, f32[64,32]{1,0:T(8,128)S(1)} %copy.13, f32[64,32]{1,0:T(8,128)S(1)} %copy.12), kind=kLoop, calls=%fused_computation | loop fusion | flops 9437184 | bytes 8413184 | tf_op jit(solution)/shard_map/convert_element_type | solution.py:472
  (25 shorter events, 0.2 us)
Async XLA Ops:
  0.6 31.2 %collective-permute-start = (bf16[576,4096]{1,0:T(8,128)(2,1)}, bf16[576,4096]{1,0:T(8,128)(2,1)}, u32[]{:S(2)}, u32[]{:S(2)}) collective-permute-start(bf16[576,4096]{1,0:T(8,128)(2,1)} %bitcast.99), channel_id=1, source_target_pairs={{0,4},{4,0},{8,12},{12,8},{1,5},{5,1},{9,13},{13,9},{2,6},{6,2},{1... | collective-permute-start | bytes 14155784 | tf_op jit(solution)/shard_map/ppermute | solution.py:397
  1.1 20.5 %copy-start.8 = (s32[256,32]{0,1:T(8,128)S(1)}, s32[256,32]{0,1:T(8,128)}, u32[]{:S(2)}) copy-start(s32[256,32]{0,1:T(8,128)} %param.12) | copy-start | bytes 98308
  15.1 60.6 %collective-permute-start.1 = (bf16[1024,256]{1,0:T(8,128)(2,1)}, bf16[1024,256]{1,0:T(8,128)(2,1)S(1)}, u32[]{:S(2)}, u32[]{:S(2)}) collective-permute-start(bf16[1024,256]{1,0:T(8,128)(2,1)} %get-tuple-element.40), channel_id=1, source_target_pairs={{0,1},{1,2},{2,3},{3,0},{4,5},{5,6},{6,7},{7,4},{8,9},{9,10},{10,1... | collective-permute-start | bytes 1572872 | tf_op jit(solution)/shard_map/ppermute | solution.py:402
  17.8 58.0 %collective-permute-start.2 = (bf16[1024,256]{1,0:T(8,128)(2,1)}, bf16[1024,256]{1,0:T(8,128)(2,1)S(1)}, u32[]{:S(2)}, u32[]{:S(2)}) collective-permute-start(bf16[1024,256]{1,0:T(8,128)(2,1)} %get-tuple-element.41), channel_id=1, source_target_pairs={{0,2},{1,3},{2,0},{3,1},{4,6},{5,7},{6,4},{7,5},{8,10},{9,11},{10,... | collective-permute-start | bytes 1572872 | tf_op jit(solution)/shard_map/ppermute | solution.py:402
  20.3 55.4 %collective-permute-start.3 = (bf16[1024,256]{1,0:T(8,128)(2,1)}, bf16[1024,256]{1,0:T(8,128)(2,1)S(1)}, u32[]{:S(2)}, u32[]{:S(2)}) collective-permute-start(bf16[1024,256]{1,0:T(8,128)(2,1)} %get-tuple-element.42), channel_id=1, source_target_pairs={{0,3},{1,0},{2,1},{3,2},{4,7},{5,4},{6,5},{7,6},{8,11},{9,8},{10,9... | collective-permute-start | bytes 1572872 | tf_op jit(solution)/shard_map/ppermute | solution.py:402
  36.8 98.6 %collective-permute-start.6 = (bf16[576,1024]{1,0:T(8,128)(2,1)}, bf16[576,1024]{1,0:T(8,128)(2,1)S(1)}, u32[]{:S(2)}, u32[]{:S(2)}) collective-permute-start(bf16[576,1024]{1,0:T(8,128)(2,1)} %get-tuple-element.84), channel_id=1, source_target_pairs={{0,8},{4,12},{8,0},{12,4},{1,9},{5,13},{9,1},{13,5},{2,10},{6,14},... | collective-permute-start | bytes 3538952 | tf_op jit(solution)/shard_map/ppermute | solution.py:428
  38.3 97.1 %collective-permute-start.5 = (bf16[576,1024]{1,0:T(8,128)(2,1)}, bf16[576,1024]{1,0:T(8,128)(2,1)}, u32[]{:S(2)}, u32[]{:S(2)}) collective-permute-start(bf16[576,1024]{1,0:T(8,128)(2,1)} %get-tuple-element.85), channel_id=1, source_target_pairs={{0,8},{4,12},{8,0},{12,4},{1,9},{5,13},{9,1},{13,5},{2,10},{6,14},... | collective-permute-start | bytes 3538952 | tf_op jit(solution)/shard_map/ppermute | solution.py:428
  75.7 0.8 copy-start.4
  75.7 0.9 copy-start.5
  75.8 1.1 copy-start.6
  76.9 60.6 %collective-permute-start.4 = (bf16[64,32,512]{2,1,0:T(8,128)(2,1)}, bf16[64,32,512]{2,1,0:T(8,128)(2,1)S(1)}, u32[]{:S(2)}, u32[]{:S(2)}) collective-permute-start(bf16[64,32,512]{2,1,0:T(8,128)(2,1)} %get-tuple-element.46), channel_id=1, source_target_pairs={{0,8},{4,12},{8,0},{12,4},{1,9},{5,13},{9,1},{13,5},{2,10},{6,14},... | collective-permute-start | bytes 6291464 | tf_op jit(solution)/shard_map/ppermute | solution.py:452
  84.0 51.4 %collective-permute-start.7 = (f32[2,32,128]{2,1,0:T(8,128)}, f32[2,32,128]{2,1,0:T(8,128)S(1)}, u32[]{:S(2)}, u32[]{:S(2)}) collective-permute-start(f32[2,32,128]{2,1,0:T(8,128)} %get-tuple-element.50), channel_id=1, source_target_pairs={{0,8},{4,12},{8,0},{12,4},{1,9},{5,13},{9,1},{13,5},{2,10},{6,14},... | collective-permute-start | bytes 98312 | tf_op jit(solution)/shard_map/ppermute | solution.py:452
  135.4 4.6 %copy-start.1 = (bf16[576,1024]{1,0:T(8,128)(2,1)}, bf16[576,1024]{1,0:T(8,128)(2,1)S(1)}, u32[]{:S(2)}) copy-start(bf16[576,1024]{1,0:T(8,128)(2,1)S(1)} %collective-permute-done.6.refs_7_) | copy-start | bytes 3538948
  135.4 4.0 %collective-permute-start.8 = (bf16[576,1024]{1,0:T(8,128)(2,1)}, bf16[576,1024]{1,0:T(8,128)(2,1)S(1)}, u32[]{:S(2)}, u32[]{:S(2)}) collective-permute-start(bf16[576,1024]{1,0:T(8,128)(2,1)} %collective-permute-done.5.refs_6_), channel_id=1, source_target_pairs={{0,4},{4,0},{8,12},{12,8},{1,5},{5,1},{9,13},{13,9},{2,6},{6,2},{1... | collective-permute-start | bytes 3538952 | tf_op jit(solution)/shard_map/ppermute | solution.py:456
  135.5 4.5 %collective-permute-start.9 = (bf16[576,1024]{1,0:T(8,128)(2,1)S(1)}, bf16[576,1024]{1,0:T(8,128)(2,1)S(1)}, u32[]{:S(2)}, u32[]{:S(2)}) collective-permute-start(bf16[576,1024]{1,0:T(8,128)(2,1)S(1)} %collective-permute-done.6.refs_7_), channel_id=1, source_target_pairs={{0,4},{4,0},{8,12},{12,8},{1,5},{5,1},{9,13},{13,9},{2,6},{6,2},{1... | collective-permute-start | bytes 3538952 | tf_op jit(solution)/shard_map/ppermute | solution.py:456
  137.5 43.7 %copy-start.7 = (f32[2,32,128]{2,1,0:T(8,128)S(1)}, f32[2,32,128]{2,1,0:T(8,128)}, u32[]{:S(2)}) copy-start(f32[2,32,128]{2,1,0:T(8,128)} %get-tuple-element.64) | copy-start | bytes 98308
  139.4 1.1 copy-start.2
  140.5 1.0 copy-start.3
  182.2 3.0 %copy-start = (bf16[64,32,512]{2,1,0:T(8,128)(2,1)S(1)}, bf16[64,32,512]{2,1,0:T(8,128)(2,1)}, u32[]{:S(2)}) copy-start(bf16[64,32,512]{2,1,0:T(8,128)(2,1)} %get-tuple-element.66) | copy-start | bytes 6291460

commit v4 on v2

--- a/solution.py
+++ b/solution.py
@@ -27,82 +27,46 @@
     return jnp.cos(angle), jnp.sin(angle)
 
 
-def index_kernel(place_ref, key_ref, query_ref, weight_ref, own_ref, *rest):
-    del place_ref
-    sent_hbm, (wide_ref, turned_ref, sent_ref, sems) = rest[:-4], rest[-4:]
-    heads, _, rows = turned_ref.shape
-    share = key_ref.shape[0]
-    step = pl.program_id(0)
-
-    @pl.when(step == 0)
+def index_kernel(key_ref, query_ref, weight_ref, out_ref, wide_ref, turned_ref):
+    heads = turned_ref.shape[0]
+    tile = key_ref.shape[0]
+
+    @pl.when(pl.program_id(0) == 0)
     def _():
         wide_ref[...] = query_ref[...].astype(jnp.float32)
         for head in range(heads):
             turned_ref[head] = wide_ref[:, head, :].T.astype(jnp.bfloat16)
 
     weight = weight_ref[...].astype(jnp.float32) * ID ** (-0.5)
-
-    def scores(first, count):
+    count = min(tile, 128)
+    for first in range(0, tile, count):
         keys = key_ref[pl.ds(first, count)]
         total = None
         for head in range(heads):
             product = jnp.dot(keys, turned_ref[head], preferred_element_type=jnp.float32)
             term = jnp.maximum(product, 0.0) * weight[head : head + 1, :]
             total = term if total is None else total + term
-        return total
-
-    count = min(share, 128)
-
-    @pl.when(step == 0)
-    def _():
-        for first in range(0, share, count):
-            own_ref[pl.ds(first, count)] = scores(first, count)
-
-    @pl.when(step > 0)
-    def _():
-        for first in range(0, share, count):
-            sent_ref[step - 1, pl.ds(first, count)] = scores(first, count).astype(jnp.bfloat16)
-
-    copies = [
-        pltpu.make_async_copy(sent_ref.at[slot], target, sems.at[slot])
-        for slot, target in enumerate(sent_hbm)
-    ]
-    for slot, copy in enumerate(copies):
-        pl.when(step == slot + 1)(copy.start)
-
-    @pl.when(step == len(copies))
-    def _():
-        for copy in copies:
-            copy.wait()
-
-
-def index_partial(index_key, index_query, index_weight, place, shards):
+        out_ref[pl.ds(first, count)] = total
+
+
+def index_partial(index_key, index_query, index_weight):
     tokens = index_key.shape[0]
     rows, heads, width = index_query.shape
-    share = tokens // shards
+    tile = min(tokens, 1024)
     return pl.pallas_call(
         index_kernel,
-        grid_spec=pltpu.PrefetchScalarGridSpec(
-            num_scalar_prefetch=1,
-            grid=(shards,),
-            in_specs=[
-                pl.BlockSpec((share, width), lambda i, at: (lax.rem(at[0] + i, shards), 0)),
-                pl.BlockSpec((rows, heads, width), lambda i, at: (0, 0, 0)),
-                pl.BlockSpec((heads, rows), lambda i, at: (0, 0)),
-            ],
-            out_specs=(
-                pl.BlockSpec((share, rows), lambda i, at: (0, 0)),
-            )
-            + (pl.BlockSpec(memory_space=pl.ANY),) * (shards - 1),
-            scratch_shapes=[
-                pltpu.VMEM((rows, heads, width), jnp.float32),
-                pltpu.VMEM((heads, width, rows), jnp.bfloat16),
-                pltpu.VMEM((shards - 1, share, rows), jnp.bfloat16),
-                pltpu.SemaphoreType.DMA((shards - 1,)),
-            ],
-        ),
-        out_shape=(jax.ShapeDtypeStruct((share, rows), jnp.float32),)
-        + (jax.ShapeDtypeStruct((share, rows), jnp.bfloat16),) * (shards - 1),
+        grid=(tokens // tile,),
+        in_specs=[
+            pl.BlockSpec((tile, width), lambda i: (i, 0)),
+            pl.BlockSpec((rows, heads, width), lambda i: (0, 0, 0)),
+            pl.BlockSpec((heads, rows), lambda i: (0, 0)),
+        ],
+        out_specs=pl.BlockSpec((tile, rows), lambda i: (i, 0)),
+        scratch_shapes=[
+            pltpu.VMEM((rows, heads, width), jnp.float32),
+            pltpu.VMEM((heads, width, rows), jnp.bfloat16),
+        ],
+        out_shape=jax.ShapeDtypeStruct((tokens, rows), jnp.float32),
         compiler_params=pltpu.CompilerParams(vmem_limit_bytes=VMEM_LIMIT),
         cost_estimate=pl.CostEstimate(
             flops=4 * tokens * rows * heads * width,
@@ -110,7 +74,7 @@
             transcendentals=0,
         ),
         name="indexer",
-    )(place, index_key, index_query, jnp.transpose(index_weight))
+    )(index_key, index_query, jnp.transpose(index_weight))
 
 
 def attend_kernel(
@@ -204,7 +168,7 @@
                     second * cosine + first * sine,
                 ],
                 axis=0,
-            ).T
+            ).astype(jnp.bfloat16).T.astype(jnp.float32)
             picked = rotated[:rows]
             for place in range(1, 128 // rows):
                 picked = jnp.where(
@@ -390,16 +354,8 @@
 
     own = jnp.transpose(cache_latent)
     peer = lax.ppermute(own, "ctx", [(i, i ^ 1) for i in range(shards)])
-    head_shards = lax.axis_size("head")
-    place = lax.axis_index("head").astype(jnp.int32).reshape(1)
-    own_scores, *sent = index_partial(index_key, index_query, index_weight, place, head_shards)
-    come = [
-        lax.ppermute(
-            sent[ahead - 1], "head", [(i, (i + ahead) % head_shards) for i in range(head_shards)]
-        )
-        for ahead in range(1, head_shards)
-    ]
-
+    partial = index_partial(index_key, index_query, index_weight)
+    index_scores = lax.psum_scatter(partial, "head", scatter_dimension=0, tiled=True)
     query = jnp.transpose(query_latent, (1, 2, 0))
     cosine, sine = rope_tables(total_rows, stretch_start)
     counts, slots = chip_slots(block_ids, me, me ^ 1, blocks, chunk, groups)
@@ -417,8 +373,6 @@
         parts.append([lax.ppermute(part, "ctx", moves) for part in attend_for(owner)])
     parts.append(attend_for(me))
 
-    come, parts[-1] = lax.optimization_barrier((come, parts[-1]))
-    index_scores = own_scores + sum(part.astype(jnp.float32) for part in come)
     peak = functools.reduce(jnp.maximum, [part[1][0] for part in parts])
     shares = [jnp.exp2((part[1][0] - peak) * EXP_SCALE) * part[1][1] for part in parts]
     whole = sum(shares)

time: 150 us -> 165 us (1.10)
  the two profiles are of different devices: /device:TPU:3 before, /device:TPU:0 now
where the time goes in v4:
time: 165 us; the launch traced here: 162 us
  Pallas kernels  138 us (84%)
  between operations  14.8 us (9%)
  other arithmetic  6.17 us (4%)
  starting transfers between devices  2.64 us (2%)
    pallas_call x2, Pallas kernels, attend(): pl.pallas_call(functools.partial(attend_kernel, chunk, groups), out_shape...  125 us
    pallas_call x1, Pallas kernels, index_partial(): pl.pallas_call(index_kernel, grid=(tokens // tile,), in_specs=[pl.BlockSp...  13.1 us
  transfers between devices with their start and end apart: 4, of which 0 were waited for; matrix products, arithmetic and copies ran while one was open for 4% of the time, Pallas kernels for 85%

profile of v4, /device:TPU:0, one launch (start us, length us, event | category | flops | bytes accessed | tf_op | source)
XLA Modules:
  0.0 162.1 jit_solution(16984713291066438137)
XLA Ops:
  7.2 0.0 reduce-scatter.2.cloned.1.call-start
  7.2 0.5 collective-permute-start
  7.7 13.1 %indexer.1 = f32[4096,256]{1,0:T(8,128)} custom-call(bf16[4096,128]{1,0:T(8,128)(2,1)} %key_ref.1, bf16[256,16,128]{2,1,0:T(8,128)(2,1)} %query_ref.1, bf16[16,256]{1,0:T(8,128)(2,1)} %bitcast.71), custom_call_target="tpu_custom_call" | custom-call | flops 8589934592 | bytes 4194304 | tf_op jit(solution)/shard_map/indexer/pallas_call | solution.py:56
  20.9 0.0 copy-start
  20.9 0.0 reduce-scatter.2.cloned.1.call-update
  21.6 0.0 copy-done
  21.6 0.1 convert_reduce_fusion
  21.7 0.6 and_select_fusion.count_ref
  22.2 0.2 fusion
  22.4 0.8 multiply_sine_fusion
  23.3 0.7 select_reduce_fusion.slot_ref
  24.0 0.0 collective-permute-done.peer_hbm
  24.0 60.7 %attend.2 = (bf16[64,32,512]{2,1,0:T(8,128)(2,1)}, f32[2,32,128]{2,1,0:T(8,128)}) custom-call(s32[1]{0:T(128)} %bitcast.1.offset_ref, s32[1,256]{1,0:T(1,128)} %and_select_fusion.count_ref, s32[24,256]{1,0:T(8,128)} %select_reduce_fusion.slot_ref, bf16[32,576,256]{2,1,0:T(8,128)(2,1)} %bitcast.66, f32[32,256]{1,0:T(8,128)} %get-tuple-element.19.cosine_ref, ...), custom_call_target="tpu_custom_call" | custom-call | flops 40000000000 | bytes 16777216 | tf_op jit(solution)/shard_map/attend/pallas_call | solution.py:295
  84.7 0.1 collective-permute-start.2
  84.8 2.0 %collective-permute-start.1 = (bf16[64,32,512]{2,1,0:T(8,128)(2,1)}, bf16[64,32,512]{2,1,0:T(8,128)(2,1)S(1)}, u32[]{:S(2)}, u32[]{:S(2)}) collective-permute-start(bf16[64,32,512]{2,1,0:T(8,128)(2,1)} %get-tuple-element.6), channel_id=1, source_target_pairs={{0,8},{4,12},{8,0},{12,4},{1,9},{5,13},{9,1},{13,5},{2,10},{6,14},... | collective-permute-start | bytes 6291464 | tf_op jit(solution)/shard_map/ppermute | solution.py:373
  86.8 64.4 %attend.3 = (bf16[64,32,512]{2,1,0:T(8,128)(2,1)}, f32[2,32,128]{2,1,0:T(8,128)}) custom-call(s32[1]{0:T(128)} %bitcast.8.offset_ref, s32[1,256]{1,0:T(1,128)} %and_select_fusion.count_ref, s32[24,256]{1,0:T(8,128)} %select_reduce_fusion.slot_ref, bf16[32,576,256]{2,1,0:T(8,128)(2,1)} %bitcast.67, f32[32,256]{1,0:T(8,128)} %get-tuple-element.19.cosine_ref, ...), custom_call_target="tpu_custom_call" | custom-call | flops 40000000000 | bytes 16777216 | tf_op jit(solution)/shard_map/attend/pallas_call | solution.py:295
  151.2 0.0 collective-permute-done.2
  151.2 0.8 fusion.18
  151.9 0.1 copy.11
  152.0 0.1 copy.12
  152.1 0.0 collective-permute-done.1
  152.1 3.2 %add_convert_fusion = bf16[64,32,512]{2,1,0:T(8,128)(2,1)} fusion(bf16[64,32,512]{2,1,0:T(8,128)(2,1)} %get-tuple-element.9, bf16[64,32,512]{2,1,0:T(8,128)(2,1)S(1)} %collective-permute-done.1, f32[64,32]{1,0:T(8,128)S(1)} %copy.12, f32[64,32]{1,0:T(8,128)S(1)} %copy.11), kind=kLoop, calls=%fused_computation | loop fusion | flops 6291456 | bytes 6307840 | tf_op jit(solution)/shard_map/convert_element_type | solution.py:383
  155.3 0.0 reduce-scatter.2.cloned.1.call-done
  (4 shorter events, 0.0 us)
Async XLA Ops:
  7.2 148.1 %reduce-scatter.2.cloned.1.call-start = ((), (), s32[]{:S(2)}) async-start(), calls=%async_computation.1 | async-start | bytes 5242880 | tf_op jit(solution)/shard_map/reduce_scatter | solution.py:358
  7.2 16.8 %collective-permute-start = (bf16[576,4096]{1,0:T(8,128)(2,1)}, bf16[576,4096]{1,0:T(8,128)(2,1)}, u32[]{:S(2)}, u32[]{:S(2)}) collective-permute-start(bf16[576,4096]{1,0:T(8,128)(2,1)} %bitcast.68), channel_id=1, source_target_pairs={{0,4},{4,0},{8,12},{12,8},{1,5},{5,1},{9,13},{13,9},{2,6},{6,2},{1... | collective-permute-start | bytes 14155784 | tf_op jit(solution)/shard_map/ppermute | solution.py:356
  20.9 0.8 copy-start
  84.7 66.5 %collective-permute-start.2 = (f32[2,32,128]{2,1,0:T(8,128)}, f32[2,32,128]{2,1,0:T(8,128)S(1)}, u32[]{:S(2)}, u32[]{:S(2)}) collective-permute-start(f32[2,32,128]{2,1,0:T(8,128)} %get-tuple-element.7), channel_id=1, source_target_pairs={{0,8},{4,12},{8,0},{12,4},{1,9},{5,13},{9,1},{13,5},{2,10},{6,14},... | collective-permute-start | bytes 98312 | tf_op jit(solution)/shard_map/ppermute | solution.py:373
  84.8 67.3 %collective-permute-start.1 = (bf16[64,32,512]{2,1,0:T(8,128)(2,1)}, bf16[64,32,512]{2,1,0:T(8,128)(2,1)S(1)}, u32[]{:S(2)}, u32[]{:S(2)}) collective-permute-start(bf16[64,32,512]{2,1,0:T(8,128)(2,1)} %get-tuple-element.6), channel_id=1, source_target_pairs={{0,8},{4,12},{8,0},{12,4},{1,9},{5,13},{9,1},{13,5},{2,10},{6,14},... | collective-permute-start | bytes 6291464 | tf_op jit(solution)/shard_map/ppermute | solution.py:373
Sparse Core Ops, SparseCore 0:
  21.0 79.1 reduce-scatter.1
